TPU v7x, 256 devices: a whole 4x4x8 slice. The times are simulated.
256 devices in a mesh: doc: 16 (over z, core), row: 4 (over x), col: 4 (over y).
Axes of the slice: x: 4, y: 4, z: 8, core: 2. Of those that a mesh axis runs over, the one named last changes fastest.
Arguments:
- tokens_in: bfloat16 [2048, 8192], P(('row', 'col'), 'doc'), may hold values from -6 to 6
- gate_weight: bfloat16 [8192, 14336], P('doc', ('row', 'col')), may hold values from -0.0625 to 0.0625
- up_weight: bfloat16 [8192, 14336], P('doc', ('row', 'col')), may hold values from -0.0625 to 0.0625
- doc_lengths: int32 [16, 8], P('doc'), may hold values from 1 to 64, 128 in all within a row
- subject_raw: int32 [16, 8], P('doc'), may hold values from 0 to 63
- residuals: bfloat16 [128, 8192], P(None, 'doc'), may hold values from -0.59765625 to 0.59765625
- regular: float32 [896], replicated, may hold values from 0.05 to 0.5
Outputs:
- panel_factor: float32 [14336, 896], P(('row', 'col'))
- updated_rhs: float32 [14336, 8192], P(('row', 'col'), 'doc')
Inputs may be any that keep to these rules, and one draw needn't show every extreme that they name: `doc_lengths`: each group's lengths sum to 128; one of them is 64.
All inputs are finite; a program needn't handle non-finite values.
Results may differ from a plain program's by a relative error of at most 0.0041.
Values may be sent and summed in bfloat16 or wider, within the bound.
A program may use at most 128 MiB of HBM per device.

v0:
```python
import jax
import jax.numpy as jnp
from jax import lax
from jax.sharding import PartitionSpec as P


def spread(array, axis, root):
    mine = lax.axis_index(axis) == root
    return lax.psum(jnp.where(mine, array, jnp.zeros_like(array)), axis)


def on_device(tokens_in, gate_weight, up_weight, doc_lengths, subject_raw, residuals, regular):
    block_index = lax.axis_index(("row", "col"))
    group_count = lax.axis_size("doc")
    gathered = lax.all_gather(tokens_in, ("row", "col"), axis=0, tiled=True)
    half_width = gate_weight.shape[1]
    group_tokens = gathered.shape[0] // group_count
    token_count = float(gathered.shape[0])
    contract_rows = (((0,), (0,)), ((), ()))
    joined_weights = jnp.concatenate([gate_weight, up_weight], axis=1)
    projected = lax.psum_scatter(
        jnp.dot(gathered, joined_weights, preferred_element_type=jnp.float32),
        "doc",
        scatter_dimension=0,
        tiled=True,
    )
    gate_part = projected[:, :half_width]
    up_part = projected[:, half_width:]
    keys_local = (jax.nn.silu(gate_part) * up_part).astype(jnp.bfloat16)
    lengths = doc_lengths[0]
    starts = jnp.cumsum(lengths, dtype=jnp.int32) - lengths
    subject_spots = starts + subject_raw[0] % lengths
    slot_index = lax.broadcasted_iota(jnp.int32, (lengths.shape[0], group_tokens), 1)
    selector = (slot_index == subject_spots[:, None]).astype(jnp.bfloat16)
    edit_local = jnp.dot(selector, keys_local, preferred_element_type=jnp.float32).astype(
        jnp.bfloat16
    )
    edit_all = lax.all_gather(edit_local, "doc", axis=0, tiled=True)
    rhs_block = lax.dot_general(
        edit_all, residuals, contract_rows, preferred_element_type=jnp.float32
    )
    panel_keys = spread(keys_local, ("row", "col"), 0)
    partial_value = lax.dot_general(
        keys_local, panel_keys, contract_rows, preferred_element_type=jnp.float32
    )
    corner_part = lax.dot_general(
        panel_keys, panel_keys, contract_rows, preferred_element_type=jnp.float32
    )
    gram_block, corner = lax.psum((partial_value, corner_part), "doc")
    gram_block = gram_block / token_count
    corner = corner / token_count
    factor = jnp.linalg.cholesky(corner + jnp.diag(regular))
    solved = jax.scipy.linalg.solve_triangular(factor, gram_block.T, lower=True).T
    l_block = jnp.where(block_index == 0, factor, solved)
    panel_local = jax.scipy.linalg.solve_triangular(factor, rhs_block, lower=True)
    panel_top = spread(panel_local, ("row", "col"), 0)
    reduced = rhs_block - jnp.dot(l_block, panel_top, precision=lax.Precision.HIGHEST)
    updated = jnp.where(block_index == 0, panel_local, reduced)
    return (l_block, updated)


def solution(mesh):
    return jax.shard_map(
        on_device,
        mesh=mesh,
        in_specs=(
            P(("row", "col"), "doc"),
            P("doc", ("row", "col")),
            P("doc", ("row", "col")),
            P("doc", None),
            P("doc", None),
            P(None, "doc"),
            P(),
        ),
        out_specs=(P(("row", "col"), None), P(("row", "col"), "doc")),
        check_vma=False,
    )
```

profile of v0, /device:TPU:4, one launch (start us, length us, event | category | flops | bytes accessed | tf_op | source)
XLA Modules:
  0.0 833.2 jit_solution(2140705690693320326)
XLA Ops:
  8.0 54.5 %all-gather.2.cloned.1.call-done = bf16[2048,512]{1,0:T(8,128)(2,1)} async-done(((bf16[128,512]{1,0:T(8,128)(2,1)}), bf16[2048,512]{1,0:T(8,128)(2,1)}) %all-gather.2.cloned.1.call-update) | async-done | bytes 2097168 | tf_op jit(solution)/shard_map/all_gather | solution.py:15
  62.5 11.4 %convolution_bitcast_fusion = f32[2048,1792]{0,1:T(8,128)} fusion(bf16[2048,512]{1,0:T(8,128)(2,1)} %all-gather.2.cloned.1.call-done, bf16[512,896]{1,0:T(8,128)(2,1)} %param.9, bf16[512,896]{1,0:T(8,128)(2,1)} %param.8), kind=kOutput, calls=%fused_computation.2 | convolution fusion | flops 3761766400 | bytes 18612224 | tf_op jit(solution)/shard_map/dot_general | solution.py:22
  73.9 90.3 %reduce-scatter.2.cloned.1.call-done = f32[128,1792]{0,1:T(8,128)} async-done(((f32[2048,1792]{0,1:T(8,128)}), f32[128,1792]{0,1:T(8,128)}) %reduce-scatter.2.cloned.1.call-update) | async-done | bytes 917520 | tf_op jit(solution)/shard_map/reduce_scatter | solution.py:21
  164.3 2.0 broadcast_select_fusion.1
  166.4 93.5 %all-reduce.6.cloned.1.call-done = bf16[128,896]{0,1:T(8,128)(2,1)} async-done(((bf16[128,896]{0,1:T(8,128)(2,1)}), bf16[128,896]{0,1:T(8,128)(2,1)}) %all-reduce.6.cloned.1.call-update) | async-done | bytes 229392 | tf_op jit(solution)/shard_map/psum | solution.py:9
  259.9 3.3 fusion.104
  263.2 2.3 fusion.105
  267.2 18.4 %all_gather.7 = bf16[128,896]{1,0:T(8,128)(2,1)S(1)} all-gather(bf16[8,896]{1,0:T(8,128)(2,1)S(1)} %convolution_convert_fusion), channel_id=1, replica_groups=mesh['doc'=16,'row'=4,'col'=4] {'doc'}, dimensions={0}, use_global_device_ids=true | all-gather | bytes 243712 | tf_op jit(solution)/shard_map/all_gather | solution.py:38
  285.6 1.7 fusion.106
  287.3 108.0 %all-reduce.10.cloned.1.call-done = (f32[896,896]{0,1:T(8,128)}, f32[896,896]{0,1:T(8,128)}) async-done(((f32[896,896]{0,1:T(8,128)}, f32[896,896]{0,1:T(8,128)}), (f32[896,896]{0,1:T(8,128)}, f32[896,896]{0,1:T(8,128)})) %all-reduce.10.cloned.1.call-update) | async-done | bytes 6422544 | tf_op jit(solution)/shard_map/psum | solution.py:49
  395.3 5.0 multiply_bitcast_fusion
  400.4 3.1 copy.10
  403.5 2.2 fusion
  405.7 1.7 copy-done.6
  407.4 11.7 %cholesky.194 = f32[128,128]{1,0:T(8,128)S(1)} custom-call(f32[128,128]{1,0:T(8,128)S(1)} %cholesky.499), custom_call_target="Cholesky" | custom-call | tf_op jit(solution)/shard_map/jit(cholesky)/cholesky | solution.py:52
  419.3 9.8 %custom-call.58 = f32[1,128,128]{1,2,0:T(8,128)S(1)} custom-call(f32[1,128,128]{2,1,0:T(8,128)S(1)} %get-tuple-element.75), custom_call_target="InvertDiagBlocksLowerTriangular" | custom-call | tf_op jit(solution)/shard_map/jit(cholesky)/cholesky | solution.py:52
  429.1 1.5 fusion.51
  431.5 1.5 convolution_subtract_fusion.4
  433.0 11.7 %cholesky.215 = f32[128,128]{1,0:T(8,128)S(1)} custom-call(f32[128,128]{1,0:T(8,128)S(1)} %cholesky.503), custom_call_target="Cholesky" | custom-call | tf_op jit(solution)/shard_map/jit(cholesky)/cholesky | solution.py:52
  444.8 10.0 %custom-call.59 = f32[1,128,128]{1,2,0:T(8,128)S(1)} custom-call(f32[1,128,128]{2,1,0:T(8,128)S(1)} %get-tuple-element.73), custom_call_target="InvertDiagBlocksLowerTriangular" | custom-call | tf_op jit(solution)/shard_map/jit(cholesky)/cholesky | solution.py:52
  456.4 2.2 convolution_subtract_fusion.5
  459.2 13.2 %cholesky.409 = f32[128,128]{1,0:T(8,128)} custom-call(f32[128,128]{1,0:T(8,128)} %cholesky.508), custom_call_target="Cholesky" | custom-call | tf_op jit(solution)/shard_map/jit(cholesky)/cholesky | solution.py:52
  472.4 1.6 copy.15
  473.9 1.5 select_reduce_fusion.4
  476.3 11.3 %custom-call.60 = f32[1,128,128]{1,2,0:T(8,128)} custom-call(f32[1,128,128]{2,1,0:T(8,128)} %get-tuple-element.71), custom_call_target="InvertDiagBlocksLowerTriangular" | custom-call | tf_op jit(solution)/shard_map/jit(cholesky)/cholesky | solution.py:52
  488.8 2.4 convolution_subtract_fusion.11
  491.2 12.7 %cholesky.428 = f32[128,128]{1,0:T(8,128)} custom-call(f32[128,128]{1,0:T(8,128)S(1)} %cholesky.513), custom_call_target="Cholesky" | custom-call | tf_op jit(solution)/shard_map/jit(cholesky)/cholesky | solution.py:52
  504.9 1.5 select_reduce_fusion.3
  506.4 10.6 %custom-call.61 = f32[1,128,128]{1,2,0:T(8,128)S(1)} custom-call(f32[1,128,128]{2,1,0:T(8,128)} %get-tuple-element.69), custom_call_target="InvertDiagBlocksLowerTriangular" | custom-call | tf_op jit(solution)/shard_map/jit(cholesky)/cholesky | solution.py:52
  517.4 2.3 convolution_subtract_fusion.13
  519.8 11.7 %cholesky.447 = f32[128,128]{1,0:T(8,128)S(1)} custom-call(f32[128,128]{1,0:T(8,128)S(1)} %cholesky.518), custom_call_target="Cholesky" | custom-call | tf_op jit(solution)/shard_map/jit(cholesky)/cholesky | solution.py:52
  532.8 10.8 %custom-call.62 = f32[1,128,128]{1,2,0:T(8,128)S(1)} custom-call(f32[1,128,128]{2,1,0:T(8,128)} %get-tuple-element.67), custom_call_target="InvertDiagBlocksLowerTriangular" | custom-call | tf_op jit(solution)/shard_map/jit(cholesky)/cholesky | solution.py:52
  543.9 2.2 convolution_subtract_fusion.14
  546.1 11.7 %cholesky.467 = f32[128,128]{1,0:T(8,128)S(1)} custom-call(f32[128,128]{1,0:T(8,128)S(1)} %cholesky.523), custom_call_target="Cholesky" | custom-call | tf_op jit(solution)/shard_map/jit(cholesky)/cholesky | solution.py:52
  558.5 9.8 %custom-call.63 = f32[1,128,128]{1,2,0:T(8,128)S(1)} custom-call(f32[1,128,128]{2,1,0:T(8,128)S(1)} %get-tuple-element.65), custom_call_target="InvertDiagBlocksLowerTriangular" | custom-call | tf_op jit(solution)/shard_map/jit(cholesky)/cholesky | solution.py:52
  568.6 1.6 convolution_subtract_fusion.15
  570.3 12.1 %cholesky.485 = f32[128,128]{1,0:T(8,128)S(1)} custom-call(f32[128,128]{1,0:T(8,128)S(1)} %convolution_subtract_fusion.15), custom_call_target="Cholesky" | custom-call | tf_op jit(solution)/shard_map/jit(cholesky)/cholesky | solution.py:52
  586.6 1.3 compare_reduce_fusion.1
  593.1 1.9 fusion.1
  595.0 24.9 %while.1 = (s32[]{:T(128)}, f32[896,896]{0,1:T(8,128)}, s32[7,2]{0,1:T(2,128)S(1)}, f32[7,128,128]{2,1,0:T(8,128)}, s32[]{:T(128)}) while((s32[]{:T(128)}, f32[896,896]{0,1:T(8,128)}, s32[7,2]{0,1:T(2,128)S(1)}, f32[7,128,128]{2,1,0:T(8,128)}, s32[]{:T(128)}) %tuple.63), condition=%wide.while_cond, body=%wide.while_body.sunk | while | flops 2 | bytes 393329 | solution.py:53
  595.6 2.2 dynamic-slice.7
  599.2 2.2 dynamic-slice.7
  602.8 2.2 dynamic-slice.7
  606.3 2.2 dynamic-slice.7
  609.9 2.2 dynamic-slice.7
  613.5 2.2 dynamic-slice.7
  617.0 2.1 dynamic-slice.7
  619.9 70.2 %custom-call.64 = f32[7,128,128]{1,2,0:T(8,128)} custom-call(f32[7,128,128]{2,1,0:T(8,128)} %get-tuple-element.9), custom_call_target="InvertDiagBlocksLowerTriangular" | custom-call | tf_op jit(solution)/shard_map/jit(_solve_triangular)/triangular_solve | solution.py:53
  690.1 1.8 constant_dynamic-update-slice_fusion.10
  692.0 1.6 convolution_subtract_fusion.3
  694.2 1.7 convolution_subtract_fusion.1
  696.6 2.1 fusion.19
  699.4 1.7 copy-done.7
  701.0 3.3 fusion.22
  713.6 1.4 broadcast_select_fusion
  715.1 2.8 constant_dynamic-update-slice_fusion.6
  717.8 3.6 convolution_subtract_fusion.2
  721.4 2.2 constant_dynamic-update-slice_fusion.5
  723.6 3.8 convolution_subtract_fusion
  727.4 1.4 convolution_dynamic-update-slice_fusion
  728.8 2.2 bitcast_select_fusion
  731.0 4.5 copy.26
  735.5 77.4 %all-reduce.8.cloned.1.call-done = f32[896,512]{1,0:T(8,128)} async-done(((f32[896,512]{1,0:T(8,128)}), f32[896,512]{1,0:T(8,128)}) %all-reduce.8.cloned.1.call-update) | async-done | bytes 1835024 | tf_op jit(solution)/shard_map/psum | solution.py:9
  812.9 13.5 %subtract_select_fusion = f32[896,512]{1,0:T(8,128)} fusion(f32[896,512]{1,0:T(8,128)} %copy-done.5, f32[896,512]{1,0:T(8,128)S(1)} %copy-done.3, f32[896,896]{0,1:T(8,128)} %bitcast_select_fusion, f32[896,512]{1,0:T(8,128)} %all-reduce.8.cloned.1.call-done, pred[]{:T(512)S(6)} %eq.26), kind=kOutput, calls=%fused_computation.23 | convolution fusion | flops 4933419008 | bytes 10551297 | tf_op jit(solution)/shard_map/dot_general | solution.py:57
  (135 shorter events, 37.3 us)
Async XLA Ops:
  7.2 278.5 %copy-start = (bf16[128,512]{1,0:T(8,128)(2,1)S(1)}, bf16[128,512]{1,0:T(8,128)(2,1)}, u32[]{:S(2)}) copy-start(bf16[128,512]{1,0:T(8,128)(2,1)} %param.12) | copy-start | bytes 393220
  7.2 55.3 %all-gather.2.cloned.1.call-start = ((), (), s32[]{:S(2)}) async-start(), calls=%async_computation.1 | async-start | bytes 2228224 | tf_op jit(solution)/shard_map/all_gather | solution.py:15
  7.9 156.4 %reduce-scatter.2.cloned.1.call-start = ((), (), s32[]{:S(2)}) async-start(), calls=%async_computation.2 | async-start | bytes 15597568 | tf_op jit(solution)/shard_map/reduce_scatter | solution.py:21
  73.9 186.0 %all-reduce.6.cloned.1.call-start = ((), (), s32[]{:S(2)}) async-start(), calls=%async_computation.3 | async-start | bytes 458752 | tf_op jit(solution)/shard_map/psum | solution.py:9
  166.3 229.0 %all-reduce.10.cloned.1.call-start = ((), (), s32[]{:S(2)}) async-start(), calls=%async_computation.5 | async-start | bytes 12845056 | tf_op jit(solution)/shard_map/psum | solution.py:49
  259.9 3.3 copy-start.11
  265.5 0.7 copy-start.18
  265.5 1.4 copy-start.17
  265.5 129.8 %copy-start.16 = (f32[896]{0:T(1024)S(1)}, f32[896]{0:T(1024)}, u32[]{:S(2)}) copy-start(f32[896]{0:T(1024)} %param.13) | copy-start | bytes 10756
  265.5 547.4 %all-reduce.8.cloned.1.call-start = ((), (), s32[]{:S(2)}) async-start(), calls=%async_computation.4 | async-start | bytes 3670016 | tf_op jit(solution)/shard_map/psum | solution.py:9
  405.7 1.7 copy-start.6
  432.9 11.9 %copy-start.13 = (f32[768,128]{1,0:T(8,128)}, f32[768,128]{1,0:T(8,128)S(1)}, u32[]{:S(2)}) copy-start(f32[768,128]{1,0:T(8,128)S(1)} %convolution_subtract_fusion.4) | copy-start | bytes 1179652
  454.8 1.0 copy-start.15
  454.8 1.1 copy-start.14
  593.1 1.9 copy-start.19
  690.1 3.5 copy-start.12
  690.1 4.1 copy-start.4
  698.7 5.7 copy-start.2
  699.3 1.7 copy-start.7
  699.3 6.4 copy-start.9
  699.4 6.4 copy-start.10
  712.3 1.3 copy-start.5
  717.8 3.6 copy-start.8
  731.0 81.9 %copy-start.3 = (f32[896,512]{1,0:T(8,128)S(1)}, f32[896,512]{1,0:T(8,128)}, u32[]{:S(2)}) copy-start(f32[896,512]{1,0:T(8,128)} %fusion.106) | copy-start | bytes 5505028
  731.0 95.5 %copy-start.1 = (bf16[128,512]{1,0:T(8,128)(2,1)S(1)}, bf16[128,512]{1,0:T(8,128)(2,1)}, u32[]{:S(2)}) copy-start(bf16[128,512]{1,0:T(8,128)(2,1)} %param.12) | copy-start | bytes 393220
Sparse Core Ops, SparseCore 0:
  10.4 51.9 all-gather.1
  74.0 90.2 reduce-scatter.1
  168.1 91.7 all-reduce.5
  265.7 129.6 all-reduce.9
  715.2 97.7 all-reduce.7
where the time goes:
time: 842 us; the launch traced here: 833 us
  waiting for transfers between devices  425 us (50%)
  other arithmetic  244 us (29%)
  matrix products  82.7 us (10%)
  local copies, waits for them, and re-layouts  44.2 us (5%)
  between operations  19.1 us (2%)
  blocking collectives  18.4 us (2%)
    psum x2, waiting for transfers between devices, spread(): return lax.psum(jnp.where(mine, array, jnp.zeros_like(array)), axis)  171 us
    another operation x27, other arithmetic, on_device(): factor = jnp.linalg.cholesky(corner + jnp.diag(regular))  158 us
    psum x1, waiting for transfers between devices, on_device(): gram_block, corner = lax.psum((partial_value, corner_part), 'doc')  108 us
    reduce_scatter x1, waiting for transfers between devices, on_device(): lax.psum_scatter(jnp.dot(gathered, joined_weights, preferred_element_type...  90.3 us
    another operation x3, other arithmetic, on_device(): jax.scipy.linalg.solve_triangular(factor, gram_block.T, lower=True)  72.7 us
    all_gather x1, waiting for transfers between devices, on_device(): gathered = lax.all_gather(tokens_in, ('row', 'col'), axis=0, tiled=True)  54.5 us
    another operation x13, matrix products, on_device(): jax.scipy.linalg.solve_triangular(factor, gram_block.T, lower=True)  26.2 us
    another operation x35, local copies, waits for them, and re-layouts  24.8 us
  transfers between devices with their start and end apart: 5, of which 5 were waited for; matrix products, arithmetic and copies ran while one was open for 3% of the time, Pallas kernels for 0%

commit v1 on v0

v1 whole, which is shorter than its diff:
```python
import functools
import math

import jax
import jax.numpy as jnp
from jax import lax
from jax.experimental import pallas as pl
from jax.experimental.pallas import tpu as pltpu
from jax.sharding import PartitionSpec as P

HI = lax.Precision.HIGHEST
MESH = pl.DeviceIdType.MESH
f32, bf16, i16, i32 = jnp.float32, jnp.bfloat16, jnp.int16, jnp.int32

ROWS, COLS, RING = 4, 4, 8
UNITS = 8
LN2 = math.log(2.0)
STEP = LN2 / 64
TOP = 32700.0


def dot(a, b, dims, precision=None):
    return lax.dot_general(a, b, (dims, ((), ())), precision=precision, preferred_element_type=f32)


def spread_row(v, k):
    return jnp.broadcast_to(v[k:k + 1, :], v.shape)


def spread_lane(v, j):
    return jnp.broadcast_to(v[:, j:j + 1], v.shape)


def factor_block(load, store):
    sub = lax.broadcasted_iota(jnp.int32, (8, 128), 0)
    lane = lax.broadcasted_iota(jnp.int32, (8, 128), 1)
    left = [load(i) for i in range(16)]
    right = [jnp.where(lane == sub + 8 * i, 1.0, 0.0).astype(f32) for i in range(16)]
    for p in range(16):
        cols = [spread_lane(left[p], 8 * p + k) for k in range(8)]
        below = {i: [spread_lane(left[i], 8 * p + k) for k in range(8)] for i in range(p + 1, 16)}
        pivots = jnp.zeros((8, 128), f32)
        a, v = left[p], right[p]
        for k in range(8):
            pivot = spread_row(cols[k], k)
            inv = 1.0 / pivot
            pivots = jnp.where(sub == k, pivot, pivots)
            ak, vk = spread_row(a, k), spread_row(v, k)
            lead = {m: spread_row(cols[m], k) for m in range(k + 1, 8)}
            mult = jnp.where(sub > k, cols[k] * inv, 0.0)
            for m in range(k + 1, 8):
                cols[m] = cols[m] - mult * lead[m]
            a = a - mult * ak
            v = v - mult * vk
            for i in range(p + 1, 16):
                part = below[i][k] * inv
                for m in range(k + 1, 8):
                    below[i][m] = below[i][m] - part * lead[m]
                left[i] = left[i] - part * ak
                right[i] = right[i] - part * vk
        scale = lax.rsqrt(pivots)
        store(p, jnp.where(lane >= sub + 8 * p, a * scale, 0.0), v * scale)


def chol_kernel(corner, regular, grams, edit0, edit, factor, rows_out, s_out, m, up, inv):
    n = corner.shape[0]
    blocks = n // 128
    r_i = lax.broadcasted_iota(jnp.int32, (128, 128), 0)
    c_i = lax.broadcasted_iota(jnp.int32, (128, 128), 1)
    m[...] = corner[...]
    for k in range(blocks):
        at = slice(k * 128, (k + 1) * 128)
        m[at, at] = m[at, at] + jnp.where(r_i == c_i, jnp.broadcast_to(regular[:, at], (128, 128)), 0.0)
    factor[...] = jnp.zeros((n, n), f32)

    def step(k, _):
        at = pl.ds(pl.multiple_of(k * 128, 128), 128)

        def load(i):
            return m[pl.ds(pl.multiple_of(k * 128 + 8 * i, 8), 8), at]

        def store(i, a, v):
            up[8 * i:8 * i + 8, :] = a
            inv[8 * i:8 * i + 8, :] = v

        factor_block(load, store)
        factor[at, at] = up[...].T
        for fixed in range(blocks):
            @pl.when(k == fixed)
            def _(fixed=fixed):
                lo, hi = fixed * 128, (fixed + 1) * 128
                li = inv[...]
                if fixed:
                    m[lo:hi, :lo] = dot(li, m[lo:hi, :lo], ((1,), (0,)), HI)
                m[lo:hi, lo:hi] = li
                if hi < n:
                    m[lo:hi, hi:] = dot(li, m[lo:hi, hi:], ((1,), (0,)), HI)
                    lt = m[lo:hi, hi:].T
                    factor[hi:, lo:hi] = lt
                    m[lo:hi, hi:] = m[lo:hi, hi:]
                    m[hi:, lo:hi] = jnp.zeros((n - hi, 128), f32)
                    for rlo in range(hi, n, 128):
                        m[rlo:rlo + 128, :] = m[rlo:rlo + 128, :] - dot(lt[rlo - hi:rlo - hi + 128], m[lo:hi, :], ((1,), (0,)), HI)
        return 0

    lax.fori_loop(0, blocks, step, 0)
    for k in range(blocks - 1):
        lo, hi = k * 128, (k + 1) * 128
        m[lo:hi, hi:] = jnp.zeros((128, n - hi), f32)
    l_rows = dot(grams[...], m[...], ((1,), (1,)), HI)
    s = dot(m[...], edit0[...], ((1,), (0,)), HI)
    s_out[...] = s
    rows_out[:, :n] = l_rows.astype(bf16)
    rows_out[:, n:] = (edit[...] - dot(l_rows, s, ((1,), (0,)), HI)).astype(bf16)


def chol_call(corner, regular, grams, edit0, edit):
    n = corner.shape[0]
    h, e = edit.shape
    return pl.pallas_call(
        chol_kernel,
        out_shape=[
            jax.ShapeDtypeStruct((n, n), f32),
            jax.ShapeDtypeStruct((h, n + e), bf16),
            jax.ShapeDtypeStruct((n, e), f32),
        ],
        scratch_shapes=[pltpu.VMEM((n, n), f32), pltpu.VMEM((128, 128), f32), pltpu.VMEM((128, 128), f32)],
        compiler_params=pltpu.CompilerParams(vmem_limit_bytes=48 << 20),
        name="panel_factor",
    )(corner, regular, grams, edit0, edit)

def place():
    doc = lax.axis_index("doc")
    return doc // 2, lax.rem(doc, 2), lax.axis_index("row"), lax.axis_index("col")


def at_device(z, core, row, col):
    return {"doc": z * 2 + core, "row": row, "col": col}


def greet(z, core, row, col, ring_steps):
    barrier = pltpu.get_barrier_semaphore()
    count = 0
    for dr in range(ROWS):
        for dc in range(COLS):
            for other in range(2):
                if dr == 0 and dc == 0 and other == 0:
                    continue
                device = at_device(z, lax.rem(core + other, 2), lax.rem(row + dr, ROWS), lax.rem(col + dc, COLS))
                pl.semaphore_signal(barrier, inc=1, device_id=device, device_id_type=MESH)
                count += 1
    for step in ring_steps:
        pl.semaphore_signal(barrier, inc=1, device_id=at_device(lax.rem(z + step, RING), core, row, col), device_id_type=MESH)
        count += 1
    return barrier, count


def remote(src, dst, send, recv, device):
    return pltpu.make_async_remote_copy(
        src_ref=src, dst_ref=dst, send_sem=send, recv_sem=recv, device_id=device, device_id_type=MESH
    )


def tile(start, size):
    return pl.ds(pl.multiple_of(start, size), size)


def project_kernel(tok, wg, wu, out, xg, wt, part, far_out, far_in, near_out, near_in,
                   xs, xr, ws, wr, fs, fr, ns, nr):
    z, core, row, col = place()
    depth, width = wg.shape
    piece = width // RING
    lanes = tok.shape[0]
    first = lax.rem(row, 2) * COLS + col
    mine = row // 2
    barrier, count = greet(z, core, row, col, (1, RING - 1))
    pl.semaphore_wait(barrier, count)

    def token_copy(i, half):
        spot = lax.rem(first - i + UNITS, UNITS)
        return remote(
            tok, xg.at[first, core], xs.at[2 * i + half], xr.at[first, core],
            at_device(z, mine, spot // COLS + 2 * half, lax.rem(spot, COLS)),
        )

    for i in range(UNITS):
        for half in range(2):
            if i == 0:
                @pl.when(jnp.logical_or(mine != half, core != mine))
                def _(i=i, half=half):
                    token_copy(i, half).start()
            else:
                token_copy(i, half).start()

    @pl.when(core == mine)
    def _():
        xg[first, core] = tok[...]

    partner = at_device(z, 1 - core, row, col)

    def weight_copy(j):
        rows = tile(j * 128, 128)
        return remote(wt.at[core, rows], wt.at[core, rows], ws.at[j], wr.at[j], partner)

    tiles = width // 128

    def turn(j, _):
        at = tile(j * 128, 128)
        wt[core, at, :] = wg[:, at].T
        weight_copy(j).start()
        wt[core, tile((j + tiles) * 128, 128), :] = wu[:, at].T
        weight_copy(j + tiles).start()
        return 0

    lax.fori_loop(0, tiles, turn, 0)

    def spot_of(u):
        return lax.rem(u + first, UNITS)

    def wait_tokens(u):
        for half in range(2):
            @pl.when(jnp.logical_not(jnp.logical_and(spot_of(u) == first, jnp.logical_and(half == core, core == mine))))
            def _(half=half):
                slot = xg.at[spot_of(u), half]
                remote(tok, slot, xs.at[0], xr.at[spot_of(u), half], partner).wait_recv()

    def project(pair):
        wait_tokens(2 * pair)
        wait_tokens(2 * pair + 1)
        x = [jnp.concatenate([xg[spot_of(2 * pair), half], xg[spot_of(2 * pair + 1), half]], axis=0) for half in range(2)]

        def chunk(j, _):
            rows = tile(j * 448, 448)
            total = dot(wt[0, rows, :], x[0], ((1,), (1,))) + dot(wt[1, rows, :], x[1], ((1,), (1,)))
            part[2 * pair, rows, :] = total[:, :lanes]
            part[2 * pair + 1, rows, :] = total[:, lanes:]
            return 0

        lax.fori_loop(0, 2 * width // 448, chunk, 0)

    def own(u, target):
        return (
            part[u, pl.ds(pl.multiple_of(target * piece, 16), piece), :],
            part[u, pl.ds(pl.multiple_of(width + target * piece, 16), piece), :],
        )

    def opened(slot):
        scale = jnp.exp(slot[2 * piece:, :].astype(i32).astype(f32)[:1] * STEP) * (1.0 / TOP)
        return (
            slot[:piece, :].astype(i32).astype(f32) * scale,
            slot[piece:2 * piece, :].astype(i32).astype(f32) * scale,
        )

    def packed(slot, g, v):
        top = jnp.maximum(jnp.max(jnp.abs(g), axis=0, keepdims=True), jnp.max(jnp.abs(v), axis=0, keepdims=True))
        grade = jnp.ceil(jnp.log(jnp.maximum(top, 1e-30)) * (1.0 / STEP)) + 1.0
        up = jnp.exp(grade * -STEP) * TOP
        slot[:piece, :] = jnp.round(g * up).astype(i32).astype(i16)
        slot[piece:2 * piece, :] = jnp.round(v * up).astype(i32).astype(i16)
        slot[2 * piece:, :] = jnp.broadcast_to(grade.astype(i32), (16, lanes)).astype(i16)

    def sign(u):
        return 1 - 2 * lax.rem(u, 2)

    def far(u, hop):
        return remote(far_out.at[u, hop], far_in.at[u, hop], fs.at[u, hop], fr.at[u, hop],
                      at_device(lax.rem(z + sign(u) + RING, RING), core, row, col))

    def near(u, hop):
        return remote(near_out.at[u, hop], near_in.at[u, hop], ns.at[u, hop], nr.at[u, hop],
                      at_device(lax.rem(z - sign(u) + RING, RING), core, row, col))

    def pass_on(u, hop):
        g, v = own(u, lax.rem(z + sign(u) * (4 - hop) + RING, RING))
        if hop:
            far(u, hop - 1).wait_recv()
            a, b = opened(far_in.at[u, hop - 1])
            g, v = g + a, v + b
        packed(far_out.at[u, hop], g, v)
        far(u, hop).start()
        if hop < 3:
            g, v = own(u, lax.rem(z - sign(u) * (3 - hop) + RING, RING))
            if hop:
                near(u, hop - 1).wait_recv()
                a, b = opened(near_in.at[u, hop - 1])
                g, v = g + a, v + b
            packed(near_out.at[u, hop], g, v)
            near(u, hop).start()

    def finish(u):
        g, v = own(u, z)
        near(u, 2).wait_recv()
        a, b = opened(near_in.at[u, 2])
        g, v = g + a, v + b
        far(u, 3).wait_recv()
        a, b = opened(far_in.at[u, 3])
        g, v = g + a, v + b
        out[:, tile(spot_of(u) * lanes, lanes)] = (g * (1.0 / (1.0 + jnp.exp(-g))) * v).astype(bf16)

    def weights_here(j, _):
        rows = tile(j * 128, 128)
        remote(wt.at[1 - core, rows], wt.at[1 - core, rows], ws.at[j], wr.at[j], partner).wait_recv()
        return 0

    lax.fori_loop(0, 2 * tiles, weights_here, 0)

    def step(g, _):
        for hop in range(1, 5):
            @pl.when(jnp.logical_and(g >= hop, g < UNITS + hop))
            def _(hop=hop):
                if hop < 4:
                    pass_on(g - hop, hop)
                else:
                    finish(g - hop)

        @pl.when(jnp.logical_and(lax.rem(g, 2) == 0, g < UNITS))
        def _():
            project(g // 2)

        @pl.when(g < UNITS)
        def _():
            pass_on(g, 0)
        return 0

    lax.fori_loop(0, UNITS + 4, step, 0)

    for i in range(UNITS):
        for half in range(2):
            if i == 0:
                @pl.when(jnp.logical_or(mine != half, core != mine))
                def _(i=i, half=half):
                    token_copy(i, half).wait_send()
            else:
                token_copy(i, half).wait_send()

    def sent(j, _):
        weight_copy(j).wait_send()
        return 0

    lax.fori_loop(0, 2 * tiles, sent, 0)

    def ring_sent(u, _):
        for hop in range(4):
            far(u, hop).wait_send()
            if hop < 3:
                near(u, hop).wait_send()
        return 0

    lax.fori_loop(0, UNITS, ring_sent, 0)


def project_call(tok, wg, wu):
    lanes, depth = tok.shape
    width = wg.shape[1]
    piece = width // RING
    rows = 2 * piece + 16
    return pl.pallas_call(
        project_kernel,
        out_shape=jax.ShapeDtypeStruct((piece, UNITS * lanes), bf16),
        in_specs=[pl.BlockSpec(memory_space=pltpu.VMEM)] * 3,
        out_specs=pl.BlockSpec(memory_space=pltpu.VMEM),
        scratch_shapes=[
            pltpu.VMEM((UNITS, 2, lanes, depth), bf16),
            pltpu.VMEM((2, 2 * width, depth), bf16),
            pltpu.VMEM((UNITS, 2 * width, lanes), f32),
            pltpu.VMEM((UNITS, 4, rows, lanes), i16),
            pltpu.VMEM((UNITS, 4, rows, lanes), i16),
            pltpu.VMEM((UNITS, 3, rows, lanes), i16),
            pltpu.VMEM((UNITS, 3, rows, lanes), i16),
            pltpu.SemaphoreType.DMA((2 * UNITS,)),
            pltpu.SemaphoreType.DMA((UNITS, 2)),
            pltpu.SemaphoreType.DMA((2 * width // 128,)),
            pltpu.SemaphoreType.DMA((2 * width // 128,)),
            pltpu.SemaphoreType.DMA((UNITS, 4)),
            pltpu.SemaphoreType.DMA((UNITS, 4)),
            pltpu.SemaphoreType.DMA((UNITS, 3)),
            pltpu.SemaphoreType.DMA((UNITS, 3)),
        ],
        compiler_params=pltpu.CompilerParams(collective_id=0, has_side_effects=True, vmem_limit_bytes=48 << 20),
        name="project_keys",
    )(tok, wg, wu)


def gram_kernel(keys, select, corner, grams, edit0, edit, k0, kb,
                ps, pr, ss, sr, zs, zr, xs, xr, hs, hr):
    z, core, row, col = place()
    piece = keys.shape[0]
    lanes = k0.shape[1] // (2 * UNITS)
    half_lanes = UNITS * lanes
    barrier, count = greet(z, core, row, col, tuple(range(1, RING)))
    pl.semaphore_wait(barrier, count)
    partner = at_device(z, 1 - core, row, col)
    mine = row // 2
    spot = lax.rem(row, 2) * COLS + col
    holder = core == mine
    origin = jnp.logical_and(row == 0, col == 0)
    own_rows = pl.ds(pl.multiple_of(z * piece, 16), piece)

    def block(c, t):
        return tile((c * UNITS + t) * lanes, lanes)

    def scatter(j):
        return remote(keys.at[:, pl.ds(j * lanes, lanes)], k0.at[own_rows, block(core, j)], ss.at[j], sr,
                      at_device(z, core, 2 * core + j // COLS, j % COLS))

    @pl.when(origin)
    def _():
        for j in range(UNITS):
            if j == 0:
                @pl.when(core == 1)
                def _():
                    scatter(0).start()
            else:
                scatter(j).start()

        @pl.when(core == 0)
        def _():
            k0[own_rows, :lanes] = keys[:, :lanes]

    own_half = tile(core * half_lanes, half_lanes)
    pair = remote(keys, kb.at[:, own_half], ps, pr, partner)
    pair.start()
    kb[:, own_half] = keys[...]

    def along(dz):
        here = k0.at[own_rows, block(core, spot)]
        return remote(here, here, zs.at[dz - 1], zr.at[dz - 1], at_device(lax.rem(z + dz, RING), core, row, col))

    def across(i):
        here = k0.at[:, block(core, spot)]
        return remote(here, here, xs.at[i - 1], xr.at[spot],
                      at_device(z, core, lax.rem(row + i // COLS, ROWS), lax.rem(col + i % COLS, COLS)))

    @pl.when(holder)
    def _():
        @pl.when(jnp.logical_not(jnp.logical_and(origin, core == 0)))
        def _():
            remote(keys.at[:, :lanes], k0.at[own_rows, block(core, spot)], ss.at[0], sr, partner).wait_recv()

        for dz in range(1, RING):
            along(dz).start()
        for dz in range(1, RING):
            there = k0.at[pl.ds(pl.multiple_of(lax.rem(z - dz + RING, RING) * piece, 16), piece), block(core, spot)]
            remote(there, there, zs.at[dz - 1], zr.at[dz - 1], partner).wait_recv()
        for i in range(1, ROWS * COLS):
            across(i).start()

    def hand_over(c, t):
        here = k0.at[:, block(c, t)]
        return remote(here, here, hs.at[t], hr.at[t], partner)

    for t in range(UNITS):
        @pl.when(jnp.logical_not(jnp.logical_and(holder, spot == t)))
        def _(t=t):
            here = k0.at[:, block(core, t)]
            remote(here, here, xs.at[0], xr.at[t], partner).wait_recv()
        hand_over(core, t).start()

    pair_in = remote(keys, kb.at[:, tile((1 - core) * half_lanes, half_lanes)], ps, pr, partner)
    pair_in.wait_recv()
    for t in range(UNITS):
        hand_over(1 - core, t).wait_recv()

    share = 1.0 / k0.shape[1]
    n = k0.shape[0]
    mid = n // 256 * 128 + 128
    nt = ((1,), (1,))
    grams[...] = dot(kb[...], k0[...], nt) * share
    corner[:mid, :] = dot(k0[:mid, :], k0[...], nt) * share
    corner[mid:, mid:] = dot(k0[mid:, :], k0[mid:, :], nt) * share
    corner[mid:, :mid] = jnp.zeros((n - mid, mid), f32)
    edit0[...] = dot(k0[...], select[...], ((1,), (0,)))
    edit[...] = dot(kb[...], select[...], ((1,), (0,)))

    pair.wait_send()
    for t in range(UNITS):
        hand_over(core, t).wait_send()

    @pl.when(origin)
    def _():
        for j in range(UNITS):
            if j == 0:
                @pl.when(core == 1)
                def _():
                    scatter(0).wait_send()
            else:
                scatter(j).wait_send()

    @pl.when(holder)
    def _():
        for dz in range(1, RING):
            along(dz).wait_send()
        for i in range(1, ROWS * COLS):
            across(i).wait_send()


def gram_call(keys, select):
    piece, half_lanes = keys.shape
    n, tokens = piece * RING, half_lanes * 2
    facts = select.shape[1]
    dma = pltpu.SemaphoreType.DMA
    return pl.pallas_call(
        gram_kernel,
        out_shape=[
            jax.ShapeDtypeStruct((n, n), f32),
            jax.ShapeDtypeStruct((piece, n), f32),
            jax.ShapeDtypeStruct((n, facts), f32),
            jax.ShapeDtypeStruct((piece, facts), f32),
        ],
        in_specs=[pl.BlockSpec(memory_space=pltpu.VMEM)] * 2,
        out_specs=[pl.BlockSpec(memory_space=pltpu.VMEM)] * 4,
        scratch_shapes=[
            pltpu.VMEM((n, tokens), bf16),
            pltpu.VMEM((piece, tokens), bf16),
            dma, dma, dma((UNITS,)), dma, dma((RING - 1,)), dma((RING - 1,)),
            dma((ROWS * COLS - 1,)), dma((UNITS,)), dma((UNITS,)), dma((UNITS,)),
        ],
        compiler_params=pltpu.CompilerParams(collective_id=1, has_side_effects=True, vmem_limit_bytes=48 << 20),
        name="gram_panel",
    )(keys, select)


def gather_kernel(rows, out, us, ur, ds, dr, hs, hr):
    z, core, row, col = place()
    piece, width = rows.shape
    half = width // 2
    barrier = pltpu.get_barrier_semaphore()
    partner = at_device(z, 1 - core, row, col)
    after = at_device(lax.rem(z + 1, RING), core, row, col)
    before = at_device(lax.rem(z + RING - 1, RING), core, row, col)
    for device in (partner, after, before):
        pl.semaphore_signal(barrier, inc=1, device_id=device, device_id_type=MESH)
    out[pl.ds(pl.multiple_of(z * piece, 16), piece), :] = rows[...]
    pl.semaphore_wait(barrier, 3)

    def slot(source, c, part=None):
        at = pl.ds(pl.multiple_of(lax.rem(source + 2 * RING, RING) * piece, 16), piece)
        if part is None:
            return out.at[at, tile(c * half, half)]
        return out.at[at, pl.ds(pl.multiple_of(c * half + part * (half // 2), half // 2), half // 2)]

    def upward(source, hop):
        here = slot(source, core, 0 if hop == 3 else None)
        return remote(here, here, us.at[hop], ur.at[hop], after)

    def downward(source, hop):
        here = slot(source, core, 1 if hop == 3 else None)
        return remote(here, here, ds.at[hop], dr.at[hop], before)

    def hand_over(source, c, index):
        here = slot(source, c)
        return remote(here, here, hs.at[index], hr.at[index], partner)

    upward(z, 0).start()
    downward(z, 0).start()
    for hop in range(1, 5):
        upward(z - hop, hop - 1).wait_recv()
        if hop < 4:
            upward(z - hop, hop).start()
        downward(z + hop, hop - 1).wait_recv()
        if hop < 4:
            downward(z + hop, hop).start()
            hand_over(z - hop, core, 2 * hop - 2).start()
            hand_over(z + hop, core, 2 * hop - 1).start()
        else:
            hand_over(z + hop, core, 6).start()
    for hop in range(1, 5):
        if hop < 4:
            hand_over(z - hop, 1 - core, 2 * hop - 2).wait_recv()
            hand_over(z + hop, 1 - core, 2 * hop - 1).wait_recv()
        else:
            hand_over(z + hop, 1 - core, 6).wait_recv()
    for hop in range(4):
        upward(z - hop, hop).wait_send()
        downward(z + hop, hop).wait_send()
    for hop in range(1, 5):
        if hop < 4:
            hand_over(z - hop, core, 2 * hop - 2).wait_send()
            hand_over(z + hop, core, 2 * hop - 1).wait_send()
        else:
            hand_over(z + hop, core, 6).wait_send()


def gather_call(rows):
    piece, width = rows.shape
    dma = pltpu.SemaphoreType.DMA
    return pl.pallas_call(
        gather_kernel,
        out_shape=jax.ShapeDtypeStruct((piece * RING, width), bf16),
        in_specs=[pl.BlockSpec(memory_space=pltpu.VMEM)],
        out_specs=pl.BlockSpec(memory_space=pltpu.VMEM),
        scratch_shapes=[dma((4,)), dma((4,)), dma((4,)), dma((4,)), dma((7,)), dma((7,))],
        compiler_params=pltpu.CompilerParams(collective_id=2, has_side_effects=True, vmem_limit_bytes=32 << 20),
        name="gather_rows",
    )(rows)


def on_device(tokens_in, gate_weight, up_weight, doc_lengths, subject_raw, residuals, regular):
    block_index = lax.axis_index(("row", "col"))
    both = lax.all_gather(jnp.concatenate([doc_lengths, subject_raw], axis=1), "doc", axis=0, tiled=True)
    groups, docs = both.shape[0], doc_lengths.shape[1]
    lengths, raw = both[:, :docs], both[:, docs:]
    tokens = tokens_in.shape[0] * ROWS * COLS
    offsets = lax.broadcasted_iota(i32, (groups, docs), 0) * (tokens // groups)
    starts = jnp.cumsum(lengths, axis=1, dtype=i32) - lengths + offsets
    spots = (starts + raw % lengths).reshape(1, -1)
    select = (lax.broadcasted_iota(i32, (tokens, groups * docs), 0) == spots).astype(bf16)
    keys = project_call(tokens_in, gate_weight, up_weight)
    corner, grams, edit0, edit = gram_call(keys, select)
    factor, rows, solved = chol_call(corner, regular.reshape(1, -1), grams, edit0, edit)
    full = gather_call(rows)
    n = factor.shape[0]
    l_block = jnp.where(block_index == 0, factor, full[:, :n].astype(f32))
    weight = jnp.where(block_index == 0, solved.astype(bf16), full[:, n:])
    updated = jnp.dot(weight, residuals, preferred_element_type=f32)
    return (l_block, updated)


def solution(mesh):
    return jax.shard_map(
        on_device,
        mesh=mesh,
        in_specs=(
            P(("row", "col"), "doc"),
            P("doc", ("row", "col")),
            P("doc", ("row", "col")),
            P("doc", None),
            P("doc", None),
            P(None, "doc"),
            P(),
        ),
        out_specs=(P(("row", "col"), None), P(("row", "col"), "doc")),
        check_vma=False,
    )
```

time: 842 us -> 235 us (0.28)
  waiting for transfers between devices: 425 us -> 0 us
  other arithmetic: 244 us -> 3.41 us
  Pallas kernels: 0 us -> 203 us
  matrix products: 82.7 us -> 1.63 us
  local copies, waits for them, and re-layouts: 44.2 us -> 5.72 us
  between operations: 19.1 us -> 0.72 us
    psum x3 -> x0, waiting for transfers between devices: 279 us -> none  [the longest x2 171 us: spread(): return lax.psum(jnp.where(mine, array, jnp.zeros_like(array)), axis)]
    another operation x31 -> x1, other arithmetic: 231 us -> 0.16 us  [on_device(): starts = jnp.cumsum(lengths, axis=1, dtype=i32) - lengths + offsets]
    pallas_call x0 -> x4, Pallas kernels: none -> 203 us  [the longest x1 73.5 us: project_call(): pl.pallas_call(project_kernel, out_shape=jax.ShapeDtypeStruct((piece, UNI...]
    reduce_scatter x1 -> x0, waiting for transfers between devices: 90.3 us -> none  [on_device(): lax.psum_scatter(jnp.dot(gathered, joined_weights, preferred_element_type...]
    all_gather x1 -> x0, waiting for transfers between devices: 54.5 us -> none  [on_device(): gathered = lax.all_gather(tokens_in, ('row', 'col'), axis=0, tiled=True)]
    another operation x38 -> x0, matrix products: 50.3 us -> none  [the longest x13 26.2 us: on_device(): jax.scipy.linalg.solve_triangular(factor, gram_block.T, lower=True)]
    dot_general x6 -> x1, matrix products: 32.4 us -> 1.63 us  [on_device(): updated = jnp.dot(weight, residuals, preferred_element_type=f32)]
    another operation x58 -> x0, local copies, waits for them, and re-layouts: 30.5 us -> none
  transfers between devices with their start and end apart: 5 -> 0, of which waited for: 5 -> 0; matrix products, arithmetic and copies ran while one was open for 3% -> 0% of each run, Pallas kernels for 0% -> 0%
where the time goes in v1:
time: 235 us; the launch traced here: 234 us
  Pallas kernels  203 us (86%)
  blocking collectives  19.8 us (8%)
  local copies, waits for them, and re-layouts  5.72 us (2%)
  other arithmetic  3.41 us (1%)
    pallas_call x1, Pallas kernels, project_call(): pl.pallas_call(project_kernel, out_shape=jax.ShapeDtypeStruct((piece, UNI...  73.5 us
    pallas_call x1, Pallas kernels, gram_call(): pl.pallas_call(gram_kernel, out_shape=[jax.ShapeDtypeStruct((n, n), f32),...  56.5 us
    pallas_call x1, Pallas kernels, chol_call(): pl.pallas_call(chol_kernel, out_shape=[jax.ShapeDtypeStruct((n, n), f32),...  50.4 us
    pallas_call x1, Pallas kernels, gather_call(): pl.pallas_call(gather_kernel, out_shape=jax.ShapeDtypeStruct((piece * RIN...  22.3 us
    all_gather x1, blocking collectives, on_device(): lax.all_gather(jnp.concatenate([doc_lengths, subject_raw], axis=1), 'doc'...  19.8 us
    unnamed x10, local copies, waits for them, and re-layouts  4.95 us

profile of v1, /device:TPU:4, one launch (start us, length us, event | category | flops | bytes accessed | tf_op | source)
XLA Modules:
  0.0 234.0 jit_solution(18121579104147084376)
XLA Ops:
  0.6 0.0 copy-start
  0.7 0.8 add_bitcast_fusion
  1.4 0.7 reshape.9.regular
  2.1 19.8 %all-gather = s32[16,1,16]{2,1,0:T(1,128)S(1)} all-gather(s32[1,1,16]{2,1,0:T(1,128)S(1)} %add_bitcast_fusion), channel_id=1, replica_groups=mesh['doc'=16,'row'=4,'col'=4] {'doc'}, dimensions={0}, use_global_device_ids=true | all-gather | bytes 1088 | tf_op jit(solution)/shard_map/all_gather | solution.py:600
  22.0 0.2 reduce_window_sum.11
  22.1 0.2 fusion.6
  22.3 0.1 eq.20
  22.4 0.0 copy-start.2
  22.4 1.2 copy-done.2
  23.6 0.0 copy-start.3
  23.6 1.2 copy-done.3
  24.8 0.0 copy-start.4
  24.8 0.9 copy-done.4
  25.7 73.5 %project_keys.1.keys = bf16[112,1024]{1,0:T(8,128)(2,1)S(1)} custom-call(bf16[128,512]{1,0:T(8,128)(2,1)S(1)} %copy-done.4, bf16[512,896]{1,0:T(8,128)(2,1)S(1)} %copy-done.2, bf16[512,896]{1,0:T(8,128)(2,1)S(1)} %copy-done.3), custom_call_target="tpu_custom_call" | custom-call | tf_op jit(solution)/shard_map/project_keys/pallas_call | solution.py:357
  99.2 0.1 fusion.select
  99.3 56.5 %gram_panel.1 = (f32[896,896]{1,0:T(8,128)S(1)}, f32[112,896]{1,0:T(8,128)S(1)}, f32[896,128]{1,0:T(8,128)S(1)}, f32[112,128]{1,0:T(8,128)S(1)}) custom-call(bf16[112,1024]{1,0:T(8,128)(2,1)S(1)} %project_keys.1.keys, bf16[2048,128]{1,0:T(8,128)(2,1)S(1)} %fusion.select), custom_call_target="tpu_custom_call" | custom-call | tf_op jit(solution)/shard_map/gram_panel/pallas_call | solution.py:502
  155.8 0.0 copy-start.1
  155.9 1.7 copy-done.1
  157.5 50.4 %panel_factor.1 = (f32[896,896]{1,0:T(8,128)S(1)}, bf16[112,1024]{1,0:T(8,128)(2,1)S(1)}, f32[896,128]{1,0:T(8,128)S(1)}) custom-call(f32[896,896]{1,0:T(8,128)} %copy-done.1, f32[1,896]{1,0:T(1,128)S(1)} %reshape.9.regular, f32[112,896]{1,0:T(8,128)S(1)} %get-tuple-element.10.grams, f32[896,128]{1,0:T(8,128)S(1)} %get-tuple-element.11.edit0, ...), custom_call_target="tpu_custom_call" | custom-call | tf_op jit(solution)/shard_map/panel_factor/pallas_call | solution.py:120
  208.0 22.3 %gather_rows.1 = bf16[896,1024]{1,0:T(8,128)(2,1)S(1)} custom-call(bf16[112,1024]{1,0:T(8,128)(2,1)S(1)} %get-tuple-element.14.rows), custom_call_target="tpu_custom_call" | custom-call | tf_op jit(solution)/shard_map/gather_rows/pallas_call | solution.py:587
  230.3 2.1 convert_select_fusion
  232.4 0.0 copy-done
  232.4 1.6 fusion.1
  (1 shorter events, 0.0 us)
Async XLA Ops:
  0.6 231.8 %copy-start = (bf16[128,512]{1,0:T(8,128)(2,1)S(1)}, bf16[128,512]{1,0:T(8,128)(2,1)}, u32[]{:S(2)}) copy-start(bf16[128,512]{1,0:T(8,128)(2,1)} %param.12) | copy-start | bytes 393220
  22.4 1.2 copy-start.2
  23.6 1.2 copy-start.3
  24.8 0.9 copy-start.4
  155.8 1.7 copy-start.1

commit v2 on v1

v2 whole, which is shorter than its diff:
```python
import functools
import math

import jax
import jax.numpy as jnp
from jax import lax
from jax.experimental import pallas as pl
from jax.experimental.pallas import tpu as pltpu
from jax.sharding import PartitionSpec as P

HI = lax.Precision.HIGHEST
MESH = pl.DeviceIdType.MESH
f32, bf16, i16, i32 = jnp.float32, jnp.bfloat16, jnp.int16, jnp.int32

ROWS, COLS, RING = 4, 4, 8
UNITS = 8
LAG = 2
LN2 = math.log(2.0)
STEP = LN2 / 64
TOP = 32700.0


def dot(a, b, dims, precision=None):
    return lax.dot_general(a, b, (dims, ((), ())), precision=precision, preferred_element_type=f32)


def spread_row(v, k):
    return jnp.broadcast_to(v[k:k + 1, :], v.shape)


def spread_lane(v, j):
    return jnp.broadcast_to(v[:, j:j + 1], v.shape)


def factor_block(load, store):
    sub = lax.broadcasted_iota(jnp.int32, (8, 128), 0)
    lane = lax.broadcasted_iota(jnp.int32, (8, 128), 1)
    left = [load(i) for i in range(16)]
    right = [jnp.where(lane == sub + 8 * i, 1.0, 0.0).astype(f32) for i in range(16)]
    for p in range(16):
        cols = [spread_lane(left[p], 8 * p + k) for k in range(8)]
        below = {i: [spread_lane(left[i], 8 * p + k) for k in range(8)] for i in range(p + 1, 16)}
        pivots = jnp.zeros((8, 128), f32)
        a, v = left[p], right[p]
        for k in range(8):
            pivot = spread_row(cols[k], k)
            inv = 1.0 / pivot
            pivots = jnp.where(sub == k, pivot, pivots)
            ak, vk = spread_row(a, k), spread_row(v, k)
            lead = {m: spread_row(cols[m], k) for m in range(k + 1, 8)}
            mult = jnp.where(sub > k, cols[k] * inv, 0.0)
            for m in range(k + 1, 8):
                cols[m] = cols[m] - mult * lead[m]
            a = a - mult * ak
            v = v - mult * vk
            for i in range(p + 1, 16):
                part = below[i][k] * inv
                for m in range(k + 1, 8):
                    below[i][m] = below[i][m] - part * lead[m]
                left[i] = left[i] - part * ak
                right[i] = right[i] - part * vk
        scale = lax.rsqrt(pivots)
        store(p, jnp.where(lane >= sub + 8 * p, a * scale, 0.0), v * scale)


def place():
    doc = lax.axis_index("doc")
    return doc // 2, lax.rem(doc, 2), lax.axis_index("row"), lax.axis_index("col")


def at_device(z, core, row, col):
    return {"doc": z * 2 + core, "row": row, "col": col}


def greet(z, core, row, col, ring_steps):
    barrier = pltpu.get_barrier_semaphore()
    count = 0
    for dr in range(ROWS):
        for dc in range(COLS):
            for other in range(2):
                if dr == 0 and dc == 0 and other == 0:
                    continue
                device = at_device(z, lax.rem(core + other, 2), lax.rem(row + dr, ROWS), lax.rem(col + dc, COLS))
                pl.semaphore_signal(barrier, inc=1, device_id=device, device_id_type=MESH)
                count += 1
    for step in ring_steps:
        pl.semaphore_signal(barrier, inc=1, device_id=at_device(lax.rem(z + step, RING), core, row, col), device_id_type=MESH)
        count += 1
    return barrier, count


def remote(src, dst, send, recv, device):
    return pltpu.make_async_remote_copy(
        src_ref=src, dst_ref=dst, send_sem=send, recv_sem=recv, device_id=device, device_id_type=MESH
    )


def tile(start, size):
    return pl.ds(pl.multiple_of(start, size), size)


def project_kernel(tok_ref, wg_ref, wu_ref, docs, out, spots_out, tok, wg, wu, spots, xg, wt, part,
                   far_out, far_in, near_out, near_in,
                   ls, qs, qr, os, orr, xs, xr, ws, wr, fs, fr, ns, nr):
    z, core, row, col = place()
    loads = [pltpu.make_async_copy(a, b, ls.at[i]) for i, (a, b) in enumerate(((tok_ref, tok), (wg_ref, wg), (wu_ref, wu)))]
    for load in loads:
        load.start()
    depth, width = wg.shape
    piece = width // RING
    lanes = tok.shape[0]
    first = lax.rem(row, 2) * COLS + col
    mine = row // 2
    barrier, count = greet(z, core, row, col, tuple(range(1, RING)))
    sub = lax.broadcasted_iota(i32, (8, 128), 0)
    lengths = docs[:8, :].astype(f32)
    raw = docs[8:, :].astype(f32)
    starts = jnp.zeros((8, 128), f32)
    for j in range(7):
        starts = starts + jnp.where(sub > j, jnp.broadcast_to(lengths[j:j + 1, :], (8, 128)), 0.0)
    wrapped = raw - lengths * jnp.floor((raw + 0.5) / lengths)
    spots[core, z] = starts + wrapped + ((z * 2 + core) * lanes).astype(f32)
    pl.semaphore_wait(barrier, count)

    def spot_copy(dz):
        here = spots.at[core, z]
        return remote(here, here, qs.at[dz - 1], qr.at[dz - 1], at_device(lax.rem(z + dz, RING), core, row, col))

    loads[0].wait()

    def token_copy(i, half):
        spot = lax.rem(first - i + UNITS, UNITS)
        return remote(
            tok, xg.at[first, core], xs.at[2 * i + half], xr.at[first, core],
            at_device(z, mine, spot // COLS + 2 * half, lax.rem(spot, COLS)),
        )

    def start_tokens(waves):
        for i in waves:
            for half in range(2):
                if i == 0:
                    @pl.when(jnp.logical_or(mine != half, core != mine))
                    def _(i=i, half=half):
                        token_copy(i, half).start()
                else:
                    token_copy(i, half).start()

    start_tokens((0, 1))

    @pl.when(core == mine)
    def _():
        xg[first, core] = tok[...]

    partner = at_device(z, 1 - core, row, col)

    def weight_copy(j):
        rows = tile(j * 128, 128)
        return remote(wt.at[core, rows], wt.at[core, rows], ws.at[j], wr.at[j], partner)

    tiles = width // 128
    loads[1].wait()
    loads[2].wait()

    def turn(j, _):
        at = tile(j * 128, 128)
        wt[core, at, :] = wg[:, at].T
        weight_copy(j).start()
        wt[core, tile((j + tiles) * 128, 128), :] = wu[:, at].T
        weight_copy(j + tiles).start()
        return 0

    lax.fori_loop(0, tiles, turn, 0)
    start_tokens((2, 3))
    for dz in range(1, RING):
        spot_copy(dz).start()

    def spot_of(u):
        return lax.rem(u + first, UNITS)

    def wait_tokens(u):
        for half in range(2):
            @pl.when(jnp.logical_not(jnp.logical_and(spot_of(u) == first, jnp.logical_and(half == core, core == mine))))
            def _(half=half):
                slot = xg.at[spot_of(u), half]
                remote(tok, slot, xs.at[0], xr.at[spot_of(u), half], partner).wait_recv()

    def project(pair):
        wait_tokens(2 * pair)
        wait_tokens(2 * pair + 1)
        x = [jnp.concatenate([xg[spot_of(2 * pair), half], xg[spot_of(2 * pair + 1), half]], axis=0) for half in range(2)]

        def chunk(j, _):
            rows = tile(j * 448, 448)
            total = dot(wt[0, rows, :], x[0], ((1,), (1,))) + dot(wt[1, rows, :], x[1], ((1,), (1,)))
            part[2 * pair, rows, :] = total[:, :lanes]
            part[2 * pair + 1, rows, :] = total[:, lanes:]
            return 0

        lax.fori_loop(0, 2 * width // 448, chunk, 0)

    def own(u, target):
        return (
            part[u, pl.ds(pl.multiple_of(target * piece, 16), piece), :],
            part[u, pl.ds(pl.multiple_of(width + target * piece, 16), piece), :],
        )

    def opened(slot):
        scale = jnp.exp(slot[2 * piece:, :].astype(i32).astype(f32)[:1] * STEP) * (1.0 / TOP)
        return (
            slot[:piece, :].astype(i32).astype(f32) * scale,
            slot[piece:2 * piece, :].astype(i32).astype(f32) * scale,
        )

    def packed(slot, g, v):
        top = jnp.maximum(jnp.max(jnp.abs(g), axis=0, keepdims=True), jnp.max(jnp.abs(v), axis=0, keepdims=True))
        grade = jnp.ceil(jnp.log(jnp.maximum(top, 1e-30)) * (1.0 / STEP)) + 1.0
        up = jnp.exp(grade * -STEP) * TOP
        slot[:piece, :] = jnp.round(g * up).astype(i32).astype(i16)
        slot[piece:2 * piece, :] = jnp.round(v * up).astype(i32).astype(i16)
        slot[2 * piece:, :] = jnp.broadcast_to(grade.astype(i32), (16, lanes)).astype(i16)

    def sign(u):
        return 1 - 2 * lax.rem(u, 2)

    def far(u, hop):
        return remote(far_out.at[u, hop], far_in.at[u, hop], fs.at[u, hop], fr.at[u, hop],
                      at_device(lax.rem(z + sign(u) + RING, RING), core, row, col))

    def near(u, hop):
        return remote(near_out.at[u, hop], near_in.at[u, hop], ns.at[u, hop], nr.at[u, hop],
                      at_device(lax.rem(z - sign(u) + RING, RING), core, row, col))

    def pass_on(u, hop):
        g, v = own(u, lax.rem(z + sign(u) * (4 - hop) + RING, RING))
        if hop:
            far(u, hop - 1).wait_recv()
            a, b = opened(far_in.at[u, hop - 1])
            g, v = g + a, v + b
        packed(far_out.at[u, hop], g, v)
        far(u, hop).start()
        if hop < 3:
            g, v = own(u, lax.rem(z - sign(u) * (3 - hop) + RING, RING))
            if hop:
                near(u, hop - 1).wait_recv()
                a, b = opened(near_in.at[u, hop - 1])
                g, v = g + a, v + b
            packed(near_out.at[u, hop], g, v)
            near(u, hop).start()

    def finish(u):
        g, v = own(u, z)
        near(u, 2).wait_recv()
        a, b = opened(near_in.at[u, 2])
        g, v = g + a, v + b
        far(u, 3).wait_recv()
        a, b = opened(far_in.at[u, 3])
        g, v = g + a, v + b
        out[spot_of(u)] = (g * (1.0 / (1.0 + jnp.exp(-g))) * v).astype(bf16)

    def weights_here(j, _):
        rows = tile(j * 128, 128)
        remote(wt.at[1 - core, rows], wt.at[1 - core, rows], ws.at[j], wr.at[j], partner).wait_recv()
        return 0

    lax.fori_loop(0, 2 * tiles, weights_here, 0)

    def step(g, _):
        for hop in range(1, 5):
            @pl.when(jnp.logical_and(g >= LAG * hop, g < UNITS + LAG * hop))
            def _(hop=hop):
                if hop < 4:
                    pass_on(g - LAG * hop, hop)
                else:
                    finish(g - LAG * hop)

        @pl.when(jnp.logical_and(lax.rem(g, 2) == 0, g < UNITS))
        def _():
            project(g // 2)

        @pl.when(g < UNITS)
        def _():
            pass_on(g, 0)

        @pl.when(g == 0)
        def _():
            start_tokens((4, 5))

        @pl.when(g == 2)
        def _():
            start_tokens((6, 7))
        return 0

    lax.fori_loop(0, UNITS + 4 * LAG, step, 0)

    for dz in range(1, RING):
        there = spots.at[core, lax.rem(z - dz + RING, RING)]
        remote(there, there, qs.at[dz - 1], qr.at[dz - 1], partner).wait_recv()
    over = remote(spots.at[core], spots.at[core], os, orr, partner)
    over.start()
    remote(spots.at[1 - core], spots.at[1 - core], os, orr, partner).wait_recv()
    for group in range(2 * RING):
        spots_out[group * 8:(group + 1) * 8, :] = spots[group % 2, group // 2]
    over.wait_send()
    for dz in range(1, RING):
        spot_copy(dz).wait_send()

    for i in range(UNITS):
        for half in range(2):
            if i == 0:
                @pl.when(jnp.logical_or(mine != half, core != mine))
                def _(i=i, half=half):
                    token_copy(i, half).wait_send()
            else:
                token_copy(i, half).wait_send()

    def sent(j, _):
        weight_copy(j).wait_send()
        return 0

    lax.fori_loop(0, 2 * tiles, sent, 0)

    def ring_sent(u, _):
        for hop in range(4):
            far(u, hop).wait_send()
            if hop < 3:
                near(u, hop).wait_send()
        return 0

    lax.fori_loop(0, UNITS, ring_sent, 0)


def project_call(tok, wg, wu, docs):
    lanes, depth = tok.shape
    width = wg.shape[1]
    piece = width // RING
    rows = 2 * piece + 16
    return pl.pallas_call(
        project_kernel,
        out_shape=[jax.ShapeDtypeStruct((UNITS, piece, lanes), bf16), jax.ShapeDtypeStruct((16 * RING, 128), f32)],
        in_specs=[pl.BlockSpec(memory_space=pl.ANY)] * 3 + [pl.BlockSpec(memory_space=pltpu.VMEM)],
        out_specs=[pl.BlockSpec(memory_space=pltpu.VMEM)] * 2,
        scratch_shapes=[
            pltpu.VMEM((lanes, depth), bf16),
            pltpu.VMEM((depth, width), bf16),
            pltpu.VMEM((depth, width), bf16),
            pltpu.VMEM((2, RING, 8, 128), f32),
            pltpu.VMEM((UNITS, 2, lanes, depth), bf16),
            pltpu.VMEM((2, 2 * width, depth), bf16),
            pltpu.VMEM((UNITS, 2 * width, lanes), f32),
            pltpu.VMEM((UNITS, 4, rows, lanes), i16),
            pltpu.VMEM((UNITS, 4, rows, lanes), i16),
            pltpu.VMEM((UNITS, 3, rows, lanes), i16),
            pltpu.VMEM((UNITS, 3, rows, lanes), i16),
            pltpu.SemaphoreType.DMA((3,)),
            pltpu.SemaphoreType.DMA((RING - 1,)),
            pltpu.SemaphoreType.DMA((RING - 1,)),
            pltpu.SemaphoreType.DMA,
            pltpu.SemaphoreType.DMA,
            pltpu.SemaphoreType.DMA((2 * UNITS,)),
            pltpu.SemaphoreType.DMA((UNITS, 2)),
            pltpu.SemaphoreType.DMA((2 * width // 128,)),
            pltpu.SemaphoreType.DMA((2 * width // 128,)),
            pltpu.SemaphoreType.DMA((UNITS, 4)),
            pltpu.SemaphoreType.DMA((UNITS, 4)),
            pltpu.SemaphoreType.DMA((UNITS, 3)),
            pltpu.SemaphoreType.DMA((UNITS, 3)),
        ],
        compiler_params=pltpu.CompilerParams(collective_id=0, has_side_effects=True, vmem_limit_bytes=48 << 20),
        name="project_keys",
    )(tok, wg, wu, docs)


def factor_kernel(keys, spots, regular, factor, inv_hi, inv_lo, solved, g_all, e_all,
                  k0, kb, select, m, up, inv, grams, edit0, edit,
                  ps, pr, ss, sr, zs, zr, xs, xr, hs, hr, gs, gr, es, er, os, orr):
    z, core, row, col = place()
    piece, lanes = keys.shape[1:]
    n = k0.shape[1]
    tokens = 2 * UNITS * lanes
    barrier, count = greet(z, core, row, col, tuple(range(1, RING)))
    pl.semaphore_wait(barrier, count)
    partner = at_device(z, 1 - core, row, col)
    mine = row // 2
    spot = lax.rem(row, 2) * COLS + col
    holder = core == mine
    origin = jnp.logical_and(row == 0, col == 0)

    def rows_of(zz):
        return pl.ds(pl.multiple_of(zz * piece, 16), piece)

    def scatter(j):
        return remote(keys.at[j], k0.at[core * UNITS + j, rows_of(z)], ss.at[j], sr,
                      at_device(z, core, 2 * core + j // COLS, j % COLS))

    @pl.when(origin)
    def _():
        for j in range(UNITS):
            if j == 0:
                @pl.when(core == 1)
                def _():
                    scatter(0).start()
            else:
                scatter(j).start()

        @pl.when(core == 0)
        def _():
            k0[0, rows_of(z), :] = keys[0]

    pair = remote(keys, kb.at[pl.ds(core * UNITS, UNITS)], ps, pr, partner)
    pair.start()
    for j in range(UNITS):
        kb[core * UNITS + j] = keys[j]

    def along(dz):
        here = k0.at[core * UNITS + spot, rows_of(z)]
        return remote(here, here, zs.at[dz - 1], zr.at[dz - 1], at_device(lax.rem(z + dz, RING), core, row, col))

    def across(i):
        here = k0.at[core * UNITS + spot]
        return remote(here, here, xs.at[i - 1], xr.at[spot],
                      at_device(z, core, lax.rem(row + i // COLS, ROWS), lax.rem(col + i % COLS, COLS)))

    @pl.when(holder)
    def _():
        @pl.when(jnp.logical_not(jnp.logical_and(origin, core == 0)))
        def _():
            remote(keys.at[0], k0.at[core * UNITS + spot, rows_of(z)], ss.at[0], sr, partner).wait_recv()

        for dz in range(1, RING):
            along(dz).start()
        for dz in range(1, RING):
            there = k0.at[core * UNITS + spot, rows_of(lax.rem(z - dz + RING, RING))]
            remote(there, there, zs.at[dz - 1], zr.at[dz - 1], partner).wait_recv()
        for i in range(1, ROWS * COLS):
            across(i).start()

    lane = lax.broadcasted_iota(i32, (128, 128), 1)
    for b in range(2 * UNITS):
        select[b] = jnp.where(lane + b * lanes == spots[...].astype(i32), 1.0, 0.0).astype(bf16)
    m[...] = jnp.zeros((n, n), f32)
    grams[...] = jnp.zeros(grams.shape, f32)
    edit0[...] = jnp.zeros(edit0.shape, f32)
    edit[...] = jnp.zeros(edit.shape, f32)
    mid = n // 256 * 128 + 128
    nt = ((1,), (1,))

    def hand_over(c, t):
        here = k0.at[c * UNITS + t]
        return remote(here, here, hs.at[t], hr.at[t], partner)

    def add_pair(c, q):
        b = c * UNITS + 2 * q
        a = jnp.concatenate([k0[b], k0[b + 1]], axis=1)
        own = jnp.concatenate([kb[b], kb[b + 1]], axis=1)
        hot = jnp.concatenate([select[b], select[b + 1]], axis=1)
        m[:mid, :] = m[:mid, :] + dot(a[:mid], a, nt)
        m[mid:, mid:] = m[mid:, mid:] + dot(a[mid:], a[mid:], nt)
        grams[...] = grams[...] + dot(own, a, nt)
        edit0[...] = edit0[...] + dot(a, hot, nt)
        edit[...] = edit[...] + dot(own, hot, nt)

    remote(keys, kb.at[pl.ds((1 - core) * UNITS, UNITS)], ps, pr, partner).wait_recv()

    def near_pair(q, _):
        for j in range(2):
            t = 2 * q + j

            @pl.when(jnp.logical_not(jnp.logical_and(holder, spot == t)))
            def _():
                here = k0.at[core * UNITS + t]
                remote(here, here, xs.at[0], xr.at[t], partner).wait_recv()
            hand_over(core, t).start()
        add_pair(core, q)
        return 0

    lax.fori_loop(0, UNITS // 2, near_pair, 0)

    def far_pair(q, _):
        for j in range(2):
            hand_over(1 - core, 2 * q + j).wait_recv()
        add_pair(1 - core, q)
        return 0

    lax.fori_loop(0, UNITS // 2, far_pair, 0)

    share = 1.0 / tokens
    top = jnp.max(jnp.abs(grams[...]), axis=1, keepdims=True) * share
    grade = jnp.ceil(jnp.log(jnp.maximum(top, 1e-30)) * (1.0 / STEP)) + 1.0
    scaled = jnp.round(grams[...] * (jnp.exp(grade * -STEP) * (TOP * share))).astype(i32).astype(i16)
    half = g_all.shape[3]

    @pl.when(core == 0)
    def _():
        g_all[0, z] = scaled[:, :half]

    @pl.when(core == 1)
    def _():
        g_all[1, z, :, :n - half] = scaled[:, half:]
        g_all[1, z, :, n - half:] = jnp.broadcast_to(grade.astype(i32), (piece, 2 * half - n)).astype(i16)

    e_all[z] = edit[...].astype(bf16)

    def give(dz):
        there = at_device(lax.rem(z + dz, RING), core, row, col)
        g, e = g_all.at[core, z], e_all.at[z]
        return (remote(g, g, gs.at[dz - 1], gr.at[dz - 1], there), remote(e, e, es.at[dz - 1], er.at[dz - 1], there))

    def take(dz):
        source = lax.rem(z - dz + RING, RING)
        g, e = g_all.at[core, source], e_all.at[source]
        return (remote(g, g, gs.at[dz - 1], gr.at[dz - 1], partner), remote(e, e, es.at[dz - 1], er.at[dz - 1], partner))

    for dz in range(1, RING):
        for copy in give(dz):
            copy.start()
    over = remote(g_all.at[core], g_all.at[core], os, orr, partner)

    blocks = n // 128
    r_i = lax.broadcasted_iota(i32, (128, 128), 0)
    c_i = lax.broadcasted_iota(i32, (128, 128), 1)
    m[...] = m[...] * share
    for k in range(blocks):
        at = slice(k * 128, (k + 1) * 128)
        m[at, at] = m[at, at] + jnp.where(r_i == c_i, jnp.broadcast_to(regular[:, at], (128, 128)), 0.0)
    factor[...] = jnp.zeros((n, n), f32)

    def step(k, _):
        at = pl.ds(pl.multiple_of(k * 128, 128), 128)

        def load(i):
            return m[pl.ds(pl.multiple_of(k * 128 + 8 * i, 8), 8), at]

        def store(i, a, v):
            up[8 * i:8 * i + 8, :] = a
            inv[8 * i:8 * i + 8, :] = v

        factor_block(load, store)
        factor[at, at] = up[...].T

        @pl.when(k == blocks - 2)
        def _():
            for dz in range(1, RING):
                for copy in take(dz):
                    copy.wait_recv()
            over.start()

        for fixed in range(blocks):
            @pl.when(k == fixed)
            def _(fixed=fixed):
                lo, hi = fixed * 128, (fixed + 1) * 128
                li = inv[...]
                if fixed:
                    m[lo:hi, :lo] = dot(li, m[lo:hi, :lo], ((1,), (0,)), HI)
                m[lo:hi, lo:hi] = li
                if hi < n:
                    m[lo:hi, hi:] = dot(li, m[lo:hi, hi:], ((1,), (0,)), HI)
                    lt = m[lo:hi, hi:].T
                    factor[hi:, lo:hi] = lt
                    for rlo in range(hi, n, 128):
                        rows = slice(rlo, rlo + 128)
                        cut = lt[rlo - hi:rlo - hi + 128]
                        if fixed:
                            m[rows, :lo] = m[rows, :lo] - dot(cut, m[lo:hi, :lo], ((1,), (0,)), HI)
                        m[rows, lo:hi] = -dot(cut, li, ((1,), (0,)), HI)
                        m[rows, rlo:] = m[rows, rlo:] - dot(cut, m[lo:hi, rlo:], ((1,), (0,)), HI)
        return 0

    lax.fori_loop(0, blocks, step, 0)
    for k in range(blocks - 1):
        lo, hi = k * 128, (k + 1) * 128
        m[lo:hi, hi:] = jnp.zeros((128, n - hi), f32)
    solved[...] = dot(m[...], edit0[...], ((1,), (0,)), HI)
    whole, rest = split(m[...])
    inv_hi[...] = whole
    inv_lo[...] = rest

    remote(g_all.at[1 - core], g_all.at[1 - core], os, orr, partner).wait_recv()
    over.wait_send()
    for dz in range(1, RING):
        for copy in give(dz):
            copy.wait_send()
    pair.wait_send()
    for t in range(UNITS):
        hand_over(core, t).wait_send()

    @pl.when(origin)
    def _():
        for j in range(UNITS):
            if j == 0:
                @pl.when(core == 1)
                def _():
                    scatter(0).wait_send()
            else:
                scatter(j).wait_send()

    @pl.when(holder)
    def _():
        for dz in range(1, RING):
            along(dz).wait_send()
        for i in range(1, ROWS * COLS):
            across(i).wait_send()


def split(a):
    whole = a.astype(bf16)
    return whole, (a - whole.astype(f32)).astype(bf16)


def factor_call(keys, spots, regular):
    units, piece, lanes = keys.shape
    n, blocks = piece * RING, 2 * units
    facts = spots.shape[0]
    dma = pltpu.SemaphoreType.DMA
    vmem = pl.BlockSpec(memory_space=pltpu.VMEM)
    return pl.pallas_call(
        factor_kernel,
        out_shape=[
            jax.ShapeDtypeStruct((n, n), f32),
            jax.ShapeDtypeStruct((n, n), bf16),
            jax.ShapeDtypeStruct((n, n), bf16),
            jax.ShapeDtypeStruct((n, facts), f32),
            jax.ShapeDtypeStruct((2, RING, piece, 512), i16),
            jax.ShapeDtypeStruct((RING, piece, facts), bf16),
        ],
        in_specs=[vmem] * 3,
        out_specs=[vmem] * 6,
        scratch_shapes=[
            pltpu.VMEM((blocks, n, lanes), bf16),
            pltpu.VMEM((blocks, piece, lanes), bf16),
            pltpu.VMEM((blocks, facts, lanes), bf16),
            pltpu.VMEM((n, n), f32),
            pltpu.VMEM((128, 128), f32),
            pltpu.VMEM((128, 128), f32),
            pltpu.VMEM((piece, n), f32),
            pltpu.VMEM((n, facts), f32),
            pltpu.VMEM((piece, facts), f32),
            dma, dma, dma((UNITS,)), dma, dma((RING - 1,)), dma((RING - 1,)),
            dma((ROWS * COLS - 1,)), dma((UNITS,)), dma((UNITS,)), dma((UNITS,)),
            dma((RING - 1,)), dma((RING - 1,)), dma((RING - 1,)), dma((RING - 1,)), dma, dma,
        ],
        compiler_params=pltpu.CompilerParams(collective_id=1, has_side_effects=True, vmem_limit_bytes=52 << 20),
        name="panel_factor",
    )(keys, spots, regular)


def finish_kernel(first, g, e, factor, inv_hi, inv_lo, solved, solved_rows, res, l_out, u_out):
    n = factor.shape[1]
    parts, piece = g.shape[1:3]
    rows = parts * piece
    nt, nn = ((1,), (1,)), ((1,), (0,))

    def send(weight):
        a, b = split(weight)
        u_out[...] = dot(a, res[...], nn) + dot(b, res[...], nn)

    @pl.when(first[0] == 0)
    def _():
        l_out[...] = factor[...]
        send(solved_rows[...])

    @pl.when(first[0] != 0)
    def _():
        whole = jnp.concatenate([jnp.concatenate([g[0, i], g[1, i]], axis=1) for i in range(parts)], axis=0).astype(i32)
        scale = jnp.exp(whole[:, n:n + 1].astype(f32) * STEP) * (1.0 / TOP)
        whole = whole[:, :n]
        high = lax.shift_right_arithmetic(whole, 8)
        low = (whole - high * 256).astype(f32).astype(bf16)
        high = high.astype(f32).astype(bf16)
        for lo in range(0, n, 256):
            hi = min(lo + 256, n)
            at = slice(lo, hi)
            a, b = inv_hi[at, :hi], inv_lo[at, :hi]
            big = dot(high[:, :hi], a, nt) + dot(high[:, :hi], b, nt)
            l_out[:, at] = (big * 256.0 + dot(low[:, :hi], a, nt)) * scale
        a, b = split(l_out[...])
        c, d = split(solved[...])
        ends = jnp.concatenate([e[i] for i in range(parts)], axis=0).astype(f32)
        send(ends - (dot(a, c, nn) + dot(a, d, nn) + dot(b, c, nn)))


def finish_call(first, g, e, factor, inv_hi, inv_lo, solved, res):
    n, facts = solved.shape
    piece, width = g.shape[2:]
    parts = 2
    rows = parts * piece
    full = lambda *shape: pl.BlockSpec(shape, lambda i: (0,) * len(shape))
    return pl.pallas_call(
        finish_kernel,
        grid=(RING // parts,),
        out_shape=[jax.ShapeDtypeStruct((n, n), f32), jax.ShapeDtypeStruct((n, res.shape[1]), f32)],
        in_specs=[
            pl.BlockSpec(memory_space=pltpu.SMEM),
            pl.BlockSpec((2, parts, piece, width), lambda i: (0, i, 0, 0)),
            pl.BlockSpec((parts, piece, facts), lambda i: (i, 0, 0)),
            pl.BlockSpec((rows, n), lambda i: (i, 0)),
            full(n, n),
            full(n, n),
            full(n, facts),
            pl.BlockSpec((rows, facts), lambda i: (i, 0)),
            full(*res.shape),
        ],
        out_specs=[pl.BlockSpec((rows, n), lambda i: (i, 0)), pl.BlockSpec((rows, res.shape[1]), lambda i: (i, 0))],
        compiler_params=pltpu.CompilerParams(vmem_limit_bytes=40 << 20),
        name="panel_rows",
    )(first, g, e, factor, inv_hi, inv_lo, solved, solved, res)


def on_device(tokens_in, gate_weight, up_weight, doc_lengths, subject_raw, residuals, regular):
    docs = jnp.broadcast_to(jnp.concatenate([doc_lengths, subject_raw], axis=1).reshape(-1, 1), (16, 128))
    keys, spots = project_call(tokens_in, gate_weight, up_weight, docs)
    factor, inv_hi, inv_lo, solved, g_all, e_all = factor_call(keys, spots, regular.reshape(1, -1))
    block_index = lax.axis_index(("row", "col")).astype(i32).reshape(1)
    return tuple(finish_call(block_index, g_all, e_all, factor, inv_hi, inv_lo, solved, residuals))


def solution(mesh):
    return jax.shard_map(
        on_device,
        mesh=mesh,
        in_specs=(
            P(("row", "col"), "doc"),
            P("doc", ("row", "col")),
            P("doc", ("row", "col")),
            P("doc", None),
            P("doc", None),
            P(None, "doc"),
            P(),
        ),
        out_specs=(P(("row", "col"), None), P(("row", "col"), "doc")),
        check_vma=False,
    )
```

time: 235 us -> 191 us (0.81)
  Pallas kernels: 203 us -> 179 us
  blocking collectives: 19.8 us -> 0 us
  local copies, waits for them, and re-layouts: 5.72 us -> 10.3 us
  other arithmetic: 3.41 us -> 0.75 us
    pallas_call x4 -> x3, Pallas kernels: 203 us -> 179 us  [the longest x1 97.9 us: factor_call(): pl.pallas_call(factor_kernel, out_shape=[jax.ShapeDtypeStruct((n, n), f32...]
    all_gather x1 -> x0, blocking collectives: 19.8 us -> none  [on_device(): lax.all_gather(jnp.concatenate([doc_lengths, subject_raw], axis=1), 'doc'...]
    unnamed x10 -> x16, local copies, waits for them, and re-layouts: 4.95 us -> 9.5 us
where the time goes in v2:
time: 191 us; the launch traced here: 190 us
  Pallas kernels  179 us (94%)
  local copies, waits for them, and re-layouts  10.3 us (5%)
    pallas_call x1, Pallas kernels, factor_call(): pl.pallas_call(factor_kernel, out_shape=[jax.ShapeDtypeStruct((n, n), f32...  97.9 us
    pallas_call x1, Pallas kernels, project_call(): pl.pallas_call(project_kernel, out_shape=[jax.ShapeDtypeStruct((UNITS, pi...  71.9 us
    unnamed x16, local copies, waits for them, and re-layouts  9.5 us
    pallas_call x1, Pallas kernels, finish_call(): pl.pallas_call(finish_kernel, grid=(RING // parts,), out_shape=[jax.Shape...  8.79 us

profile of v2, /device:TPU:4, one launch (start us, length us, event | category | flops | bytes accessed | tf_op | source)
XLA Modules:
  0.0 190.3 jit_solution(8936214801827723052)
XLA Ops:
  0.6 0.7 add_bitcast_fusion
  1.4 0.7 reshape.13.regular
  2.1 0.1 broadcast_in_dim.8.docs
  2.1 0.0 copy-start.4
  2.1 1.2 copy-done.4
  3.3 0.0 copy-start.5
  3.3 1.2 copy-done.5
  4.5 0.0 copy-start.7
  4.5 0.9 copy-done.7
  5.4 0.0 copy-start.6
  5.4 71.9 %project_keys.1 = (bf16[8,112,128]{2,1,0:T(8,128)(2,1)S(1)}, f32[128,128]{1,0:T(8,128)S(1)}) custom-call(bf16[128,512]{1,0:T(8,128)(2,1)S(1)} %copy-done.7, bf16[512,896]{1,0:T(8,128)(2,1)S(1)} %copy-done.4, bf16[512,896]{1,0:T(8,128)(2,1)S(1)} %copy-done.5, s32[16,128]{1,0:T(8,128)S(1)} %broadcast_in_dim.8.docs), custom_call_target="tpu_custom_call" | custom-call | tf_op jit(solution)/shard_map/project_keys/pallas_call | solution.py:337
  77.3 97.9 %panel_factor.1 = (f32[896,896]{1,0:T(8,128)}, bf16[896,896]{1,0:T(8,128)(2,1)}, bf16[896,896]{1,0:T(8,128)(2,1)}, f32[896,128]{1,0:T(8,128)S(1)}, s16[2,8,112,5...) custom-call(bf16[8,112,128]{2,1,0:T(8,128)(2,1)S(1)} %get-tuple-element.10.keys, ...), custom_call_target="tpu_custom_call" | custom-call | tf_op jit(solution)/shard_map/panel_factor/pallas_call | solution.py:615
  175.2 0.0 copy-done.6
  175.2 0.0 copy-start
  175.2 1.9 copy-done
  177.1 0.0 copy-start.1
  177.1 1.5 copy-done.1
  178.6 0.0 copy-start.2
  178.6 1.4 copy-done.2
  180.1 0.0 copy-start.3
  180.1 1.4 copy-done.3
  181.5 8.8 %panel_rows.1 = (f32[896,896]{1,0:T(8,128)}, f32[896,512]{1,0:T(8,128)}) custom-call(s32[1]{0:T(128)} %bitcast.first, s16[2,8,112,512]{3,2,1,0:T(8,128)(2,1)S(1)} %copy-done.1, bf16[8,112,128]{2,1,0:T(8,128)(2,1)S(1)} %get-tuple-element.13.e, f32[896,896]{1,0:T(8,128)S(1)} %copy-done, bf16[896,896]{1,0:T(8,128)(2,1)S(1)} %copy-done.2, ...), custom_call_target="tpu_custom_call" | custom-call | tf_op jit(solution)/shard_map/panel_rows/pallas_call | solution.py:687
Async XLA Ops:
  2.1 1.2 copy-start.4
  3.3 1.2 copy-start.5
  4.5 0.9 copy-start.7
  5.4 169.8 %copy-start.6 = (bf16[128,512]{1,0:T(8,128)(2,1)S(1)}, bf16[128,512]{1,0:T(8,128)(2,1)}, u32[]{:S(2)}) copy-start(bf16[128,512]{1,0:T(8,128)(2,1)} %res.1) | copy-start | bytes 393220
  175.2 1.9 %copy-start = (f32[896,896]{1,0:T(8,128)S(1)}, f32[896,896]{1,0:T(8,128)}, u32[]{:S(2)}) copy-start(f32[896,896]{1,0:T(8,128)} %get-tuple-element.14.factor) | copy-start | bytes 9633796
  177.1 1.5 copy-start.1
  178.6 1.4 copy-start.2
  180.1 1.4 copy-start.3

commit v3 on v2

v3 whole, which is shorter than its diff:
```python
import functools
import math

import jax
import jax.numpy as jnp
from jax import lax
from jax.experimental import pallas as pl
from jax.experimental.pallas import tpu as pltpu
from jax.sharding import PartitionSpec as P

HI = lax.Precision.HIGHEST
MESH = pl.DeviceIdType.MESH
f32, bf16, i16, i32 = jnp.float32, jnp.bfloat16, jnp.int16, jnp.int32

ROWS, COLS, RING = 4, 4, 8
UNITS = 8
LAG = 2
LN2 = math.log(2.0)
STEP = LN2 / 64
TOP = 32700.0


def dot(a, b, dims, precision=None):
    return lax.dot_general(a, b, (dims, ((), ())), precision=precision, preferred_element_type=f32)


def spread_row(v, k):
    return jnp.broadcast_to(v[k:k + 1, :], v.shape)


def spread_lane(v, j):
    return jnp.broadcast_to(v[:, j:j + 1], v.shape)


def factor_block(load, store):
    sub = lax.broadcasted_iota(jnp.int32, (8, 128), 0)
    lane = lax.broadcasted_iota(jnp.int32, (8, 128), 1)
    left = [load(i) for i in range(16)]
    right = [jnp.where(lane == sub + 8 * i, 1.0, 0.0).astype(f32) for i in range(16)]
    for p in range(16):
        cols = [spread_lane(left[p], 8 * p + k) for k in range(8)]
        below = {i: [spread_lane(left[i], 8 * p + k) for k in range(8)] for i in range(p + 1, 16)}
        pivots = jnp.zeros((8, 128), f32)
        a, v = left[p], right[p]
        for k in range(8):
            pivot = spread_row(cols[k], k)
            inv = 1.0 / pivot
            pivots = jnp.where(sub == k, pivot, pivots)
            ak, vk = spread_row(a, k), spread_row(v, k)
            lead = {m: spread_row(cols[m], k) for m in range(k + 1, 8)}
            mult = jnp.where(sub > k, cols[k] * inv, 0.0)
            for m in range(k + 1, 8):
                cols[m] = cols[m] - mult * lead[m]
            a = a - mult * ak
            v = v - mult * vk
            for i in range(p + 1, 16):
                part = below[i][k] * inv
                for m in range(k + 1, 8):
                    below[i][m] = below[i][m] - part * lead[m]
                left[i] = left[i] - part * ak
                right[i] = right[i] - part * vk
        scale = lax.rsqrt(pivots)
        store(p, jnp.where(lane >= sub + 8 * p, a * scale, 0.0), v * scale)


def place():
    doc = lax.axis_index("doc")
    return doc // 2, lax.rem(doc, 2), lax.axis_index("row"), lax.axis_index("col")


def at_device(z, core, row, col):
    return {"doc": z * 2 + core, "row": row, "col": col}


def greet(z, core, row, col, ring_steps):
    barrier = pltpu.get_barrier_semaphore()
    count = 0
    for dr in range(ROWS):
        for dc in range(COLS):
            for other in range(2):
                if dr == 0 and dc == 0 and other == 0:
                    continue
                device = at_device(z, lax.rem(core + other, 2), lax.rem(row + dr, ROWS), lax.rem(col + dc, COLS))
                pl.semaphore_signal(barrier, inc=1, device_id=device, device_id_type=MESH)
                count += 1
    for step in ring_steps:
        pl.semaphore_signal(barrier, inc=1, device_id=at_device(lax.rem(z + step, RING), core, row, col), device_id_type=MESH)
        count += 1
    return barrier, count


def remote(src, dst, send, recv, device):
    return pltpu.make_async_remote_copy(
        src_ref=src, dst_ref=dst, send_sem=send, recv_sem=recv, device_id=device, device_id_type=MESH
    )


def tile(start, size):
    return pl.ds(pl.multiple_of(start, size), size)


def whole_kernel(tok_ref, wg_ref, wu_ref, docs, regular, res, l_out, u_out,
                 tok, wg, wu, spots, xg, wt, part, far_out, far_in, near_out, near_in,
                 k0, kb, select, m, up, inv, grams, edit0, edit, g_all, e_all, inv_hi, inv_lo,
                 ls, qs, qr, os, orr, t1, t2, t3, xr, ws, wr, fs, fr, ns, nr,
                 ps, pr, ss, sr, zs, zr, b1, b2, b3, br, hs, hr, gs, gr, es, er, vs, vr):
    z, core, row, col = place()
    loads = [pltpu.make_async_copy(a, b, ls.at[i]) for i, (a, b) in enumerate(((tok_ref, tok), (wg_ref, wg), (wu_ref, wu)))]
    for load in loads:
        load.start()
    depth, width = wg.shape
    piece = width // RING
    lanes = tok.shape[0]
    odd = lax.rem(row, 2)
    first = odd * COLS + col
    mine = row // 2
    holder = core == mine
    origin = jnp.logical_and(row == 0, col == 0)

    def rows_of(zz):
        return pl.ds(pl.multiple_of(zz * piece, 16), piece)

    def in_row(step):
        return at_device(z, core, row, lax.rem(col + step, COLS))

    def in_column(step):
        return at_device(z, core, lax.rem(row + step, ROWS), col)

    barrier, count = greet(z, core, row, col, tuple(range(1, RING)))
    sub = lax.broadcasted_iota(i32, (8, 128), 0)
    lengths = docs[:8, :].astype(f32)
    raw = docs[8:, :].astype(f32)
    starts = jnp.zeros((8, 128), f32)
    for j in range(7):
        starts = starts + jnp.where(sub > j, jnp.broadcast_to(lengths[j:j + 1, :], (8, 128)), 0.0)
    wrapped = raw - lengths * jnp.floor((raw + 0.5) / lengths)
    spots[core, z] = starts + wrapped + ((z * 2 + core) * lanes).astype(f32)
    pl.semaphore_wait(barrier, count)

    def spot_copy(dz):
        here = spots.at[core, z]
        return remote(here, here, qs.at[dz - 1], qr.at[dz - 1], at_device(lax.rem(z + dz, RING), core, row, col))

    loads[0].wait()

    def token_first(step):
        slot = xg.at[first, core]
        x_way = at_device(z, mine, lax.rem(row + step * (1 - core), ROWS), lax.rem(col + step * core, COLS))
        return remote(tok, slot, t1.at[step], xr.at[first, core], x_way)

    for step in (0, 3, 2, 1):
        if step:
            token_first(step).start()
        else:
            @pl.when(core != mine)
            def _():
                token_first(0).start()

    @pl.when(holder)
    def _():
        xg[first, core] = tok[...]

    partner = at_device(z, 1 - core, row, col)

    def weight_copy(j):
        rows = tile(j * 128, 128)
        return remote(wt.at[core, rows], wt.at[core, rows], ws.at[j], wr.at[j], partner)

    tiles = width // 128
    loads[1].wait()
    loads[2].wait()

    def turn(j, _):
        at = tile(j * 128, 128)
        wt[core, at, :] = wg[:, at].T
        weight_copy(j).start()
        wt[core, tile((j + tiles) * 128, 128), :] = wu[:, at].T
        weight_copy(j + tiles).start()
        return 0

    def here_tokens(t, half):
        slot = xg.at[t, half]
        remote(slot, slot, t1.at[0], xr.at[t, half], partner).wait_recv()

    def token_row(s, step):
        slot = xg.at[s * COLS + col, 0]
        return remote(slot, slot, t2.at[s, step - 1], xr.at[s * COLS + col, 0], in_row(step))

    def token_column(j, step):
        t = odd * COLS + lax.rem(col + j, COLS)
        return remote(xg.at[t, 1], xg.at[t, 1], t3.at[j, step - 1], xr.at[t, 1], in_column(step))

    lax.fori_loop(0, 3, turn, 0)
    for s in range(2):
        @pl.when(jnp.logical_not(jnp.logical_and(holder, jnp.logical_and(core == 0, odd == s))))
        def _(s=s):
            here_tokens(s * COLS + col, 0)
        for step in (3, 2, 1):
            token_row(s, step).start()

    @pl.when(holder)
    def _():
        for j in range(COLS):
            if j == 0:
                @pl.when(core == 0)
                def _():
                    here_tokens(first, 1)
            else:
                here_tokens(odd * COLS + lax.rem(col + j, COLS), 1)
            for step in (1, 3, 2):
                token_column(j, step).start()

    lax.fori_loop(3, tiles, turn, 0)
    for dz in range(1, RING):
        spot_copy(dz).start()

    def spot_of(u):
        return lax.rem(u, 2) * COLS + lax.rem(col + u // 2, COLS)

    def settled(t, half):
        if half == 0:
            return lax.rem(t, COLS) == col
        return jnp.logical_and(holder, t // COLS == odd)

    def wait_tokens(u):
        for half in range(2):
            @pl.when(jnp.logical_not(settled(spot_of(u), half)))
            def _(half=half):
                here_tokens(spot_of(u), half)

    def project(pair):
        wait_tokens(2 * pair)
        wait_tokens(2 * pair + 1)
        x = [jnp.concatenate([xg[spot_of(2 * pair), half], xg[spot_of(2 * pair + 1), half]], axis=0) for half in range(2)]

        def chunk(j, _):
            rows = tile(j * 448, 448)
            total = dot(wt[0, rows, :], x[0], ((1,), (1,))) + dot(wt[1, rows, :], x[1], ((1,), (1,)))
            part[2 * pair, rows, :] = total[:, :lanes]
            part[2 * pair + 1, rows, :] = total[:, lanes:]
            return 0

        lax.fori_loop(0, 2 * width // 448, chunk, 0)

    def own(u, target):
        return (
            part[u, pl.ds(pl.multiple_of(target * piece, 16), piece), :],
            part[u, pl.ds(pl.multiple_of(width + target * piece, 16), piece), :],
        )

    def opened(slot):
        scale = jnp.exp(slot[2 * piece:, :].astype(i32).astype(f32)[:1] * STEP) * (1.0 / TOP)
        return (
            slot[:piece, :].astype(i32).astype(f32) * scale,
            slot[piece:2 * piece, :].astype(i32).astype(f32) * scale,
        )

    def packed(slot, g, v):
        top = jnp.maximum(jnp.max(jnp.abs(g), axis=0, keepdims=True), jnp.max(jnp.abs(v), axis=0, keepdims=True))
        grade = jnp.ceil(jnp.log(jnp.maximum(top, 1e-30)) * (1.0 / STEP)) + 1.0
        up = jnp.exp(grade * -STEP) * TOP
        slot[:piece, :] = jnp.round(g * up).astype(i32).astype(i16)
        slot[piece:2 * piece, :] = jnp.round(v * up).astype(i32).astype(i16)
        slot[2 * piece:, :] = jnp.broadcast_to(grade.astype(i32), (16, lanes)).astype(i16)

    def sign(u):
        return 1 - 2 * lax.rem(u, 2)

    def far(u, hop):
        return remote(far_out.at[u, hop], far_in.at[u, hop], fs.at[u, hop], fr.at[u, hop],
                      at_device(lax.rem(z + sign(u) + RING, RING), core, row, col))

    def near(u, hop):
        return remote(near_out.at[u, hop], near_in.at[u, hop], ns.at[u, hop], nr.at[u, hop],
                      at_device(lax.rem(z - sign(u) + RING, RING), core, row, col))

    def pass_on(u, hop):
        g, v = own(u, lax.rem(z + sign(u) * (4 - hop) + RING, RING))
        if hop:
            far(u, hop - 1).wait_recv()
            a, b = opened(far_in.at[u, hop - 1])
            g, v = g + a, v + b
        packed(far_out.at[u, hop], g, v)
        far(u, hop).start()
        if hop < 3:
            g, v = own(u, lax.rem(z - sign(u) * (3 - hop) + RING, RING))
            if hop:
                near(u, hop - 1).wait_recv()
                a, b = opened(near_in.at[u, hop - 1])
                g, v = g + a, v + b
            packed(near_out.at[u, hop], g, v)
            near(u, hop).start()

    def scatter(t):
        return remote(kb.at[core * UNITS + t], k0.at[core * UNITS + t, rows_of(z)], ss.at[t], sr,
                      at_device(z, core, 2 * core + t // COLS, lax.rem(t, COLS)))

    def finish(u):
        g, v = own(u, z)
        near(u, 2).wait_recv()
        a, b = opened(near_in.at[u, 2])
        g, v = g + a, v + b
        far(u, 3).wait_recv()
        a, b = opened(far_in.at[u, 3])
        g, v = g + a, v + b
        t = spot_of(u)
        kb[core * UNITS + t] = (g * (1.0 / (1.0 + jnp.exp(-g))) * v).astype(bf16)
        home = jnp.logical_and(core == 0, t == 0)

        @pl.when(jnp.logical_and(origin, home))
        def _():
            k0[0, rows_of(z), :] = kb[0]

        @pl.when(jnp.logical_and(origin, jnp.logical_not(home)))
        def _():
            scatter(t).start()

    def weights_here(j, _):
        rows = tile(j * 128, 128)
        remote(wt.at[1 - core, rows], wt.at[1 - core, rows], ws.at[j], wr.at[j], partner).wait_recv()
        return 0

    lax.fori_loop(0, 2 * tiles, weights_here, 0)

    def step(g, _):
        for hop in range(1, 5):
            @pl.when(jnp.logical_and(g >= LAG * hop, g < UNITS + LAG * hop))
            def _(hop=hop):
                if hop < 4:
                    pass_on(g - LAG * hop, hop)
                else:
                    finish(g - LAG * hop)

        @pl.when(jnp.logical_and(lax.rem(g, 2) == 0, g < UNITS))
        def _():
            project(g // 2)

        @pl.when(g < UNITS)
        def _():
            pass_on(g, 0)

        return 0

    lax.fori_loop(0, UNITS + 4 * LAG, step, 0)

    own_keys = kb.at[pl.ds(core * UNITS, UNITS)]
    pair = remote(own_keys, own_keys, ps, pr, partner)
    pair.start()
    n, tokens = k0.shape[1], 2 * UNITS * lanes
    half_rows = n // 2

    def along(dz):
        here = k0.at[core * UNITS + first, rows_of(z)]
        return remote(here, here, zs.at[dz - 1], zr.at[dz - 1], at_device(lax.rem(z + dz, RING), core, row, col))

    def half_of(t, half):
        return k0.at[core * UNITS + t, pl.ds(half * half_rows, half_rows)]

    def block_first(half, step):
        here = half_of(first, half)
        return remote(here, here, b1.at[half, step - 1], br.at[first, half], in_row(step) if half else in_column(step))

    def block_row(s, step):
        t = s * COLS + col
        return remote(half_of(t, 0), half_of(t, 0), b2.at[s, step - 1], br.at[t, 0], in_row(step))

    def block_column(j, step):
        t = odd * COLS + lax.rem(col + j, COLS)
        return remote(half_of(t, 1), half_of(t, 1), b3.at[j, step - 1], br.at[t, 1], in_column(step))

    def here_block(t, half):
        remote(half_of(t, half), half_of(t, half), b1.at[0, 0], br.at[t, half], partner).wait_recv()

    @pl.when(holder)
    def _():
        @pl.when(jnp.logical_not(jnp.logical_and(origin, core == 0)))
        def _():
            here = k0.at[core * UNITS + first, rows_of(z)]
            remote(here, here, ss.at[0], sr, partner).wait_recv()

        for dz in range(1, RING):
            along(dz).start()

    for dz in range(1, RING):
        there = spots.at[core, lax.rem(z - dz + RING, RING)]
        remote(there, there, qs.at[dz - 1], qr.at[dz - 1], partner).wait_recv()
    over = remote(spots.at[core], spots.at[core], os, orr, partner)
    over.start()
    remote(spots.at[1 - core], spots.at[1 - core], os, orr, partner).wait_recv()
    over.wait_send()
    for dz in range(1, RING):
        spot_copy(dz).wait_send()

    lane = lax.broadcasted_iota(i32, (128, 128), 1)
    spots_row = jnp.concatenate([spots[group % 2, group // 2] for group in range(2 * RING)], axis=0).astype(i32)
    for b in range(2 * UNITS):
        select[b] = jnp.where(lane + b * lanes == spots_row, 1.0, 0.0).astype(bf16)
    m[...] = jnp.zeros((n, n), f32)
    grams[...] = jnp.zeros(grams.shape, f32)
    edit0[...] = jnp.zeros(edit0.shape, f32)
    edit[...] = jnp.zeros(edit.shape, f32)

    @pl.when(holder)
    def _():
        for dz in range(1, RING):
            there = k0.at[core * UNITS + first, rows_of(lax.rem(z - dz + RING, RING))]
            remote(there, there, zs.at[dz - 1], zr.at[dz - 1], partner).wait_recv()
        for step in (3, 1, 2):
            for half in range(2):
                block_first(half, step).start()

    for s in range(2):
        @pl.when(jnp.logical_not(jnp.logical_and(holder, odd == s)))
        def _(s=s):
            here_block(s * COLS + col, 0)
        for step in (3, 2, 1):
            block_row(s, step).start()

    @pl.when(holder)
    def _():
        for j in range(COLS):
            if j:
                here_block(odd * COLS + lax.rem(col + j, COLS), 1)
            for step in (1, 3, 2):
                block_column(j, step).start()

    mid = n // 256 * 128 + 128
    nt = ((1,), (1,))

    def hand_over(c, t):
        here = k0.at[c * UNITS + t]
        return remote(here, here, hs.at[t], hr.at[t], partner)

    def add_pair(c, q):
        b0, b1_ = c * UNITS + spot_of(2 * q), c * UNITS + spot_of(2 * q + 1)
        a = jnp.concatenate([k0[b0], k0[b1_]], axis=1)
        own = jnp.concatenate([kb[b0], kb[b1_]], axis=1)
        hot = jnp.concatenate([select[b0], select[b1_]], axis=1)
        m[:mid, :] = m[:mid, :] + dot(a[:mid], a, nt)
        m[mid:, mid:] = m[mid:, mid:] + dot(a[mid:], a[mid:], nt)
        grams[...] = grams[...] + dot(own, a, nt)
        edit0[...] = edit0[...] + dot(a, hot, nt)
        edit[...] = edit[...] + dot(own, hot, nt)

    their_keys = kb.at[pl.ds((1 - core) * UNITS, UNITS)]
    remote(their_keys, their_keys, ps, pr, partner).wait_recv()

    def near_pair(q, _):
        for j in range(2):
            t = spot_of(2 * q + j)
            for half in range(2):
                @pl.when(jnp.logical_not(settled(t, half)))
                def _(t=t, half=half):
                    here_block(t, half)
            hand_over(core, t).start()
        add_pair(core, q)
        return 0

    lax.fori_loop(0, UNITS // 2, near_pair, 0)

    def far_pair(q, _):
        for j in range(2):
            hand_over(1 - core, spot_of(2 * q + j)).wait_recv()
        add_pair(1 - core, q)
        return 0

    lax.fori_loop(0, UNITS // 2, far_pair, 0)

    share = 1.0 / tokens
    top = jnp.max(jnp.abs(grams[...]), axis=1, keepdims=True) * share
    grade = jnp.ceil(jnp.log(jnp.maximum(top, 1e-30)) * (1.0 / STEP)) + 1.0
    scaled = jnp.round(grams[...] * (jnp.exp(grade * -STEP) * (TOP * share))).astype(i32).astype(i16)
    half = g_all.shape[3]

    @pl.when(core == 0)
    def _():
        g_all[0, z] = scaled[:, :half]

    @pl.when(core == 1)
    def _():
        g_all[1, z, :, :n - half] = scaled[:, half:]
        g_all[1, z, :, n - half:] = jnp.broadcast_to(grade.astype(i32), (piece, 2 * half - n)).astype(i16)

    e_all[z] = edit[...].astype(bf16)

    def give(dz):
        there = at_device(lax.rem(z + dz, RING), core, row, col)
        g, e = g_all.at[core, z], e_all.at[z]
        return (remote(g, g, gs.at[dz - 1], gr.at[dz - 1], there), remote(e, e, es.at[dz - 1], er.at[dz - 1], there))

    def take(dz):
        source = lax.rem(z - dz + RING, RING)
        g, e = g_all.at[core, source], e_all.at[source]
        return (remote(g, g, gs.at[dz - 1], gr.at[dz - 1], partner), remote(e, e, es.at[dz - 1], er.at[dz - 1], partner))

    for dz in range(1, RING):
        for copy in give(dz):
            copy.start()
    give_over = remote(g_all.at[core], g_all.at[core], vs, vr, partner)

    blocks = n // 128
    r_i = lax.broadcasted_iota(i32, (128, 128), 0)
    c_i = lax.broadcasted_iota(i32, (128, 128), 1)
    m[...] = m[...] * share
    for k in range(blocks):
        at = slice(k * 128, (k + 1) * 128)
        m[at, at] = m[at, at] + jnp.where(r_i == c_i, jnp.broadcast_to(regular[:, at], (128, 128)), 0.0)
    l_out[...] = jnp.zeros((n, n), f32)

    def step(k, _):
        at = pl.ds(pl.multiple_of(k * 128, 128), 128)

        def load(i):
            return m[pl.ds(pl.multiple_of(k * 128 + 8 * i, 8), 8), at]

        def store(i, a, v):
            up[8 * i:8 * i + 8, :] = a
            inv[8 * i:8 * i + 8, :] = v

        factor_block(load, store)
        l_out[at, at] = up[...].T

        @pl.when(k == blocks - 2)
        def _():
            for dz in range(1, RING):
                for copy in take(dz):
                    copy.wait_recv()
            give_over.start()

        for fixed in range(blocks):
            @pl.when(k == fixed)
            def _(fixed=fixed):
                lo, hi = fixed * 128, (fixed + 1) * 128
                li = inv[...]
                if fixed:
                    m[lo:hi, :lo] = dot(li, m[lo:hi, :lo], ((1,), (0,)), HI)
                m[lo:hi, lo:hi] = li
                if hi < n:
                    m[lo:hi, hi:] = dot(li, m[lo:hi, hi:], ((1,), (0,)), HI)
                    lt = m[lo:hi, hi:].T
                    l_out[hi:, lo:hi] = lt
                    for rlo in range(hi, n, 128):
                        rows = slice(rlo, rlo + 128)
                        cut = lt[rlo - hi:rlo - hi + 128]
                        if fixed:
                            m[rows, :lo] = m[rows, :lo] - dot(cut, m[lo:hi, :lo], ((1,), (0,)), HI)
                        m[rows, lo:hi] = -dot(cut, li, ((1,), (0,)), HI)
                        m[rows, rlo:] = m[rows, rlo:] - dot(cut, m[lo:hi, rlo:], ((1,), (0,)), HI)
        return 0

    lax.fori_loop(0, blocks, step, 0)
    for k in range(blocks - 1):
        lo, hi = k * 128, (k + 1) * 128
        m[lo:hi, hi:] = jnp.zeros((128, n - hi), f32)
    solved = dot(m[...], edit0[...], ((1,), (0,)), HI)
    edit0[...] = solved
    whole, rest = split(m[...])
    inv_hi[...] = whole
    inv_lo[...] = rest
    remote(g_all.at[1 - core], g_all.at[1 - core], vs, vr, partner).wait_recv()
    nn = ((1,), (0,))

    def send(rows, weight):
        a, b = split(weight)
        u_out[rows, :] = dot(a, res[...], nn) + dot(b, res[...], nn)

    @pl.when(origin)
    def _():
        send(pl.ds(0, n), edit0[...])

    @pl.when(jnp.logical_not(origin))
    def _():
        c, d = split(edit0[...])

        def rows_part(i, _):
            rows = tile(i * 2 * piece, 2 * piece)
            g = jnp.concatenate([
                jnp.concatenate([g_all[0, 2 * i + s], g_all[1, 2 * i + s]], axis=1) for s in range(2)
            ], axis=0).astype(i32)
            scale = jnp.exp(g[:, n:n + 1].astype(f32) * STEP) * (1.0 / TOP)
            g = g[:, :n]
            high = lax.shift_right_arithmetic(g, 8)
            low = (g - high * 256).astype(f32).astype(bf16)
            high = high.astype(f32).astype(bf16)
            for lo in range(0, n, 256):
                hi = min(lo + 256, n)
                at = slice(lo, hi)
                a, b = inv_hi[at, :hi], inv_lo[at, :hi]
                big = dot(high[:, :hi], a, nt) + dot(high[:, :hi], b, nt)
                l_out[rows, at] = (big * 256.0 + dot(low[:, :hi], a, nt)) * scale
            a, b = split(l_out[rows, :])
            ends = jnp.concatenate([e_all[2 * i], e_all[2 * i + 1]], axis=0).astype(f32)
            send(rows, ends - (dot(a, c, nn) + dot(a, d, nn) + dot(b, c, nn)))
            return 0

        lax.fori_loop(0, RING // 2, rows_part, 0)

    give_over.wait_send()
    for dz in range(1, RING):
        for copy in give(dz):
            copy.wait_send()
    pair.wait_send()
    for t in range(UNITS):
        hand_over(core, t).wait_send()

    @pl.when(origin)
    def _():
        for t in range(UNITS):
            if t == 0:
                @pl.when(core == 1)
                def _():
                    scatter(0).wait_send()
            else:
                scatter(t).wait_send()

    for step in (1, 2, 3):
        token_first(step).wait_send()
        for s in range(2):
            token_row(s, step).wait_send()
            block_row(s, step).wait_send()

    @pl.when(core != mine)
    def _():
        token_first(0).wait_send()

    @pl.when(holder)
    def _():
        for dz in range(1, RING):
            along(dz).wait_send()
        for step in (1, 2, 3):
            for half in range(2):
                block_first(half, step).wait_send()
            for j in range(COLS):
                token_column(j, step).wait_send()
                block_column(j, step).wait_send()

    def sent(j, _):
        weight_copy(j).wait_send()
        return 0

    lax.fori_loop(0, 2 * tiles, sent, 0)

    def ring_sent(u, _):
        for hop in range(4):
            far(u, hop).wait_send()
            if hop < 3:
                near(u, hop).wait_send()
        return 0

    lax.fori_loop(0, UNITS, ring_sent, 0)


def split(a):
    whole = a.astype(bf16)
    return whole, (a - whole.astype(f32)).astype(bf16)


def whole_call(tok, wg, wu, docs, regular, res):
    lanes, depth = tok.shape
    width = wg.shape[1]
    piece = width // RING
    rows = 2 * piece + 16
    n, blocks, facts = width, 2 * UNITS, 8 * 2 * RING
    dma = pltpu.SemaphoreType.DMA
    vmem = pl.BlockSpec(memory_space=pltpu.VMEM)
    tiles = 2 * width // 128
    return pl.pallas_call(
        whole_kernel,
        out_shape=[jax.ShapeDtypeStruct((n, n), f32), jax.ShapeDtypeStruct((n, res.shape[1]), f32)],
        in_specs=[pl.BlockSpec(memory_space=pl.ANY)] * 3 + [vmem] * 3,
        out_specs=[vmem] * 2,
        scratch_shapes=[
            pltpu.VMEM((lanes, depth), bf16),
            pltpu.VMEM((depth, width), bf16),
            pltpu.VMEM((depth, width), bf16),
            pltpu.VMEM((2, RING, 8, 128), f32),
            pltpu.VMEM((UNITS, 2, lanes, depth), bf16),
            pltpu.VMEM((2, 2 * width, depth), bf16),
            pltpu.VMEM((UNITS, 2 * width, lanes), f32),
            pltpu.VMEM((UNITS, 4, rows, lanes), i16),
            pltpu.VMEM((UNITS, 4, rows, lanes), i16),
            pltpu.VMEM((UNITS, 3, rows, lanes), i16),
            pltpu.VMEM((UNITS, 3, rows, lanes), i16),
            pltpu.VMEM((blocks, n, lanes), bf16),
            pltpu.VMEM((blocks, piece, lanes), bf16),
            pltpu.VMEM((blocks, facts, lanes), bf16),
            pltpu.VMEM((n, n), f32),
            pltpu.VMEM((128, 128), f32),
            pltpu.VMEM((128, 128), f32),
            pltpu.VMEM((piece, n), f32),
            pltpu.VMEM((n, facts), f32),
            pltpu.VMEM((piece, facts), f32),
            pltpu.VMEM((2, RING, piece, 512), i16),
            pltpu.VMEM((RING, piece, facts), bf16),
            pltpu.VMEM((n, n), bf16),
            pltpu.VMEM((n, n), bf16),
            dma((3,)), dma((RING - 1,)), dma((RING - 1,)), dma, dma,
            dma((4,)), dma((2, 3)), dma((COLS, 3)), dma((UNITS, 2)), dma((tiles,)), dma((tiles,)),
            dma((UNITS, 4)), dma((UNITS, 4)), dma((UNITS, 3)), dma((UNITS, 3)),
            dma, dma, dma((UNITS,)), dma, dma((RING - 1,)), dma((RING - 1,)),
            dma((2, 3)), dma((2, 3)), dma((COLS, 3)), dma((UNITS, 2)), dma((UNITS,)), dma((UNITS,)),
            dma((RING - 1,)), dma((RING - 1,)), dma((RING - 1,)), dma((RING - 1,)), dma, dma,
        ],
        compiler_params=pltpu.CompilerParams(collective_id=0, has_side_effects=True, vmem_limit_bytes=60 << 20),
        name="panel_edit",
    )(tok, wg, wu, docs, regular, res)


def on_device(tokens_in, gate_weight, up_weight, doc_lengths, subject_raw, residuals, regular):
    docs = jnp.broadcast_to(jnp.concatenate([doc_lengths, subject_raw], axis=1).reshape(-1, 1), (16, 128))
    return tuple(whole_call(tokens_in, gate_weight, up_weight, docs, regular.reshape(1, -1), residuals))


def solution(mesh):
    return jax.shard_map(
        on_device,
        mesh=mesh,
        in_specs=(
            P(("row", "col"), "doc"),
            P("doc", ("row", "col")),
            P("doc", ("row", "col")),
            P("doc", None),
            P("doc", None),
            P(None, "doc"),
            P(),
        ),
        out_specs=(P(("row", "col"), None), P(("row", "col"), "doc")),
        check_vma=False,
    )
```

time: 191 us -> 159 us (0.83); the launches traced: 190 us -> 156 us
  Pallas kernels: 179 us -> 148 us
  local copies, waits for them, and re-layouts: 10.3 us -> 7.1 us
    pallas_call x3 -> x1, Pallas kernels: 179 us -> 148 us  [whole_call(): pl.pallas_call(whole_kernel, out_shape=[jax.ShapeDtypeStruct((n, n), f32)...]
    unnamed x16 -> x4, local copies, waits for them, and re-layouts: 9.5 us -> 5.17 us
where the time goes in v3:
time: 159 us; the launch traced here: 156 us
  Pallas kernels  148 us (93%)
  local copies, waits for them, and re-layouts  7.1 us (4%)
    pallas_call x1, Pallas kernels, whole_call(): pl.pallas_call(whole_kernel, out_shape=[jax.ShapeDtypeStruct((n, n), f32)...  148 us
    unnamed x4, local copies, waits for them, and re-layouts  5.17 us

profile of v3, /device:TPU:4, one launch (start us, length us, event | category | flops | bytes accessed | tf_op | source)
XLA Modules:
  0.0 156.0 jit_solution(5477570970937252820)
XLA Ops:
  0.6 0.7 add_bitcast_fusion
  1.4 1.3 reshape.9.regular
  2.6 0.7 broadcast_in_dim.8.docs
  3.3 147.5 %panel_edit.1 = (f32[896,896]{1,0:T(8,128)}, f32[896,512]{1,0:T(8,128)}) custom-call(bf16[128,512]{1,0:T(8,128)(2,1)} %tok_ref.1, bf16[512,896]{1,0:T(8,128)(2,1)} %wg_ref.1, bf16[512,896]{1,0:T(8,128)(2,1)} %wu_ref.1, s32[16,128]{1,0:T(8,128)} %broadcast_in_dim.8.docs, f32[1,896]{1,0:T(1,128)} %reshape.9.regular, bf16[128,512]{1,0:T(8,128)(2,1)} %res.1), custom_call_target="tpu_custom_call" | custom-call | tf_op jit(solution)/shard_map/panel_edit/pallas_call | solution.py:667
  150.8 0.0 copy-start
  150.8 3.9 %copy.11 = f32[896,896]{1,0:T(8,128)} copy(f32[896,896]{1,0:T(8,128)} %get-tuple-element.4) | data formatting | bytes 6422528
  154.8 0.0 copy-done
  154.8 1.2 copy.12
Async XLA Ops:
  150.8 3.9 %copy-start = (f32[896,512]{1,0:T(8,128)S(1)}, f32[896,512]{1,0:T(8,128)}, u32[]{:S(2)}) copy-start(f32[896,512]{1,0:T(8,128)} %get-tuple-element.5) | copy-start | bytes 5505028

commit v4 on v3

--- a/solution.py
+++ b/solution.py
@@ -14,7 +14,7 @@
 
 ROWS, COLS, RING = 4, 4, 8
 UNITS = 8
-LAG = 2
+LAG = 3
 LN2 = math.log(2.0)
 STEP = LN2 / 64
 TOP = 32700.0
@@ -99,11 +99,11 @@
     return pl.ds(pl.multiple_of(start, size), size)
 
 
-def whole_kernel(tok_ref, wg_ref, wu_ref, docs, regular, res, l_out, u_out,
+def whole_kernel(tok_ref, wg_ref, wu_ref, lengths_ref, raw_ref, regular, res, l_out, u_out,
                  tok, wg, wu, spots, xg, wt, part, far_out, far_in, near_out, near_in,
                  k0, kb, select, m, up, inv, grams, edit0, edit, g_all, e_all, inv_hi, inv_lo,
                  ls, qs, qr, os, orr, t1, t2, t3, xr, ws, wr, fs, fr, ns, nr,
-                 ps, pr, ss, sr, zs, zr, b1, b2, b3, br, hs, hr, gs, gr, es, er, vs, vr):
+                 ps, pr, ss, sr, zs, zr, b1, b2, b3, br, c1, c2, cr, hs, hr, gs, gr, es, er, vs, vr):
     z, core, row, col = place()
     loads = [pltpu.make_async_copy(a, b, ls.at[i]) for i, (a, b) in enumerate(((tok_ref, tok), (wg_ref, wg), (wu_ref, wu)))]
     for load in loads:
@@ -128,8 +128,13 @@
 
     barrier, count = greet(z, core, row, col, tuple(range(1, RING)))
     sub = lax.broadcasted_iota(i32, (8, 128), 0)
-    lengths = docs[:8, :].astype(f32)
-    raw = docs[8:, :].astype(f32)
+    square = lax.broadcasted_iota(i32, (8, 8), 0) == lax.broadcasted_iota(i32, (8, 8), 1)
+
+    def upright(ref):
+        values = jnp.broadcast_to(ref[...].astype(f32), (8, 8))
+        return jnp.broadcast_to(jnp.sum(jnp.where(square, values, 0.0), axis=1, keepdims=True), (8, 128))
+
+    lengths, raw = upright(lengths_ref), upright(raw_ref)
     starts = jnp.zeros((8, 128), f32)
     for j in range(7):
         starts = starts + jnp.where(sub > j, jnp.broadcast_to(lengths[j:j + 1, :], (8, 128)), 0.0)
@@ -368,6 +373,27 @@
         t = odd * COLS + lax.rem(col + j, COLS)
         return remote(half_of(t, 1), half_of(t, 1), b3.at[j, step - 1], br.at[t, 1], in_column(step))
 
+    def quarter(t, half, part):
+        return k0.at[core * UNITS + t, pl.ds(half * half_rows + part * (half_rows // 2), half_rows // 2)]
+
+    def onward_row(s, part):
+        t = s * COLS + lax.rem(col + (3, 1)[part], COLS)
+        here = quarter(t, 0, part)
+        return remote(here, here, c1.at[s, part], cr.at[t, 0, part], in_row((1, 3)[part]))
+
+    def onward_column(s, j, part):
+        t = s * COLS + j
+        here = quarter(t, 1, part)
+        return remote(here, here, c2.at[s, j], cr.at[t, 1, part], in_column((1, 3)[part]))
+
+    def away(s):
+        return lax.rem(row - 2 * core - s + 2 * ROWS, ROWS)
+
+    def opposite(t, half):
+        if half:
+            return away(t // COLS) == 2
+        return lax.rem(lax.rem(t, COLS) - col + COLS, COLS) == 2
+
     def here_block(t, half):
         remote(half_of(t, half), half_of(t, half), b1.at[0, 0], br.at[t, half], partner).wait_recv()
 
@@ -413,7 +439,7 @@
         @pl.when(jnp.logical_not(jnp.logical_and(holder, odd == s)))
         def _(s=s):
             here_block(s * COLS + col, 0)
-        for step in (3, 2, 1):
+        for step in (1, 3):
             block_row(s, step).start()
 
     @pl.when(holder)
@@ -421,8 +447,20 @@
         for j in range(COLS):
             if j:
                 here_block(odd * COLS + lax.rem(col + j, COLS), 1)
-            for step in (1, 3, 2):
+            for step in (1, 3):
                 block_column(j, step).start()
+
+    for s in range(2):
+        for part in range(2):
+            here_block(s * COLS + lax.rem(col + (3, 1)[part], COLS), 0)
+            onward_row(s, part).start()
+    for s in range(2):
+        for part in range(2):
+            @pl.when(away(s) == (1, 3)[part])
+            def _(s=s, part=part):
+                for j in range(COLS):
+                    here_block(s * COLS + j, 1)
+                    onward_column(s, j, part).start()
 
     mid = n // 256 * 128 + 128
     nt = ((1,), (1,))
@@ -449,9 +487,11 @@
         for j in range(2):
             t = spot_of(2 * q + j)
             for half in range(2):
-                @pl.when(jnp.logical_not(settled(t, half)))
+                @pl.when(opposite(t, half))
                 def _(t=t, half=half):
-                    here_block(t, half)
+                    for part in range(2):
+                        here = quarter(t, half, part)
+                        remote(here, here, c1.at[0, 0], cr.at[t, half, part], partner).wait_recv()
             hand_over(core, t).start()
         add_pair(core, q)
         return 0
@@ -504,7 +544,7 @@
     m[...] = m[...] * share
     for k in range(blocks):
         at = slice(k * 128, (k + 1) * 128)
-        m[at, at] = m[at, at] + jnp.where(r_i == c_i, jnp.broadcast_to(regular[:, at], (128, 128)), 0.0)
+        m[at, at] = m[at, at] + jnp.where(r_i == c_i, jnp.broadcast_to(regular[at], (128, 128)), 0.0)
     l_out[...] = jnp.zeros((n, n), f32)
 
     def step(k, _):
@@ -573,9 +613,9 @@
         c, d = split(edit0[...])
 
         def rows_part(i, _):
-            rows = tile(i * 2 * piece, 2 * piece)
+            rows = tile(i * 4 * piece, 4 * piece)
             g = jnp.concatenate([
-                jnp.concatenate([g_all[0, 2 * i + s], g_all[1, 2 * i + s]], axis=1) for s in range(2)
+                jnp.concatenate([g_all[0, 4 * i + s], g_all[1, 4 * i + s]], axis=1) for s in range(4)
             ], axis=0).astype(i32)
             scale = jnp.exp(g[:, n:n + 1].astype(f32) * STEP) * (1.0 / TOP)
             g = g[:, :n]
@@ -589,11 +629,11 @@
                 big = dot(high[:, :hi], a, nt) + dot(high[:, :hi], b, nt)
                 l_out[rows, at] = (big * 256.0 + dot(low[:, :hi], a, nt)) * scale
             a, b = split(l_out[rows, :])
-            ends = jnp.concatenate([e_all[2 * i], e_all[2 * i + 1]], axis=0).astype(f32)
+            ends = jnp.concatenate([e_all[4 * i + s] for s in range(4)], axis=0).astype(f32)
             send(rows, ends - (dot(a, c, nn) + dot(a, d, nn) + dot(b, c, nn)))
             return 0
 
-        lax.fori_loop(0, RING // 2, rows_part, 0)
+        lax.fori_loop(0, RING // 4, rows_part, 0)
 
     give_over.wait_send()
     for dz in range(1, RING):
@@ -617,7 +657,8 @@
         token_first(step).wait_send()
         for s in range(2):
             token_row(s, step).wait_send()
-            block_row(s, step).wait_send()
+            if step != 2:
+                block_row(s, step).wait_send()
 
     @pl.when(core != mine)
     def _():
@@ -632,7 +673,17 @@
                 block_first(half, step).wait_send()
             for j in range(COLS):
                 token_column(j, step).wait_send()
-                block_column(j, step).wait_send()
+                if step != 2:
+                    block_column(j, step).wait_send()
+
+    for s in range(2):
+        for part in range(2):
+            onward_row(s, part).wait_send()
+
+            @pl.when(away(s) == (1, 3)[part])
+            def _(s=s, part=part):
+                for j in range(COLS):
+                    onward_column(s, j, part).wait_send()
 
     def sent(j, _):
         weight_copy(j).wait_send()
@@ -655,7 +706,7 @@
     return whole, (a - whole.astype(f32)).astype(bf16)
 
 
-def whole_call(tok, wg, wu, docs, regular, res):
+def whole_call(tok, wg, wu, lengths, raw, regular, res):
     lanes, depth = tok.shape
     width = wg.shape[1]
     piece = width // RING
@@ -667,7 +718,7 @@
     return pl.pallas_call(
         whole_kernel,
         out_shape=[jax.ShapeDtypeStruct((n, n), f32), jax.ShapeDtypeStruct((n, res.shape[1]), f32)],
-        in_specs=[pl.BlockSpec(memory_space=pl.ANY)] * 3 + [vmem] * 3,
+        in_specs=[pl.BlockSpec(memory_space=pl.ANY)] * 3 + [vmem] * 4,
         out_specs=[vmem] * 2,
         scratch_shapes=[
             pltpu.VMEM((lanes, depth), bf16),
@@ -698,17 +749,17 @@
             dma((4,)), dma((2, 3)), dma((COLS, 3)), dma((UNITS, 2)), dma((tiles,)), dma((tiles,)),
             dma((UNITS, 4)), dma((UNITS, 4)), dma((UNITS, 3)), dma((UNITS, 3)),
             dma, dma, dma((UNITS,)), dma, dma((RING - 1,)), dma((RING - 1,)),
-            dma((2, 3)), dma((2, 3)), dma((COLS, 3)), dma((UNITS, 2)), dma((UNITS,)), dma((UNITS,)),
+            dma((2, 3)), dma((2, 3)), dma((COLS, 3)), dma((UNITS, 2)),
+            dma((2, 2)), dma((2, COLS)), dma((UNITS, 2, 2)), dma((UNITS,)), dma((UNITS,)),
             dma((RING - 1,)), dma((RING - 1,)), dma((RING - 1,)), dma((RING - 1,)), dma, dma,
         ],
         compiler_params=pltpu.CompilerParams(collective_id=0, has_side_effects=True, vmem_limit_bytes=60 << 20),
         name="panel_edit",
-    )(tok, wg, wu, docs, regular, res)
+    )(tok, wg, wu, lengths, raw, regular, res)
 
 
 def on_device(tokens_in, gate_weight, up_weight, doc_lengths, subject_raw, residuals, regular):
-    docs = jnp.broadcast_to(jnp.concatenate([doc_lengths, subject_raw], axis=1).reshape(-1, 1), (16, 128))
-    return tuple(whole_call(tokens_in, gate_weight, up_weight, docs, regular.reshape(1, -1), residuals))
+    return tuple(whole_call(tokens_in, gate_weight, up_weight, doc_lengths, subject_raw, regular, residuals))
 
 
 def solution(mesh):

time: 159 us -> 157 us (0.987)
  local copies, waits for them, and re-layouts: 7.1 us -> 5.17 us
where the time goes in v4:
time: 157 us; the launch traced here: 154 us
  Pallas kernels  149 us (95%)
  local copies, waits for them, and re-layouts  5.17 us (3%)
    pallas_call x1, Pallas kernels, whole_call(): pl.pallas_call(whole_kernel, out_shape=[jax.ShapeDtypeStruct((n, n), f32)...  149 us
    unnamed x4, local copies, waits for them, and re-layouts  5.17 us

profile of v4, /device:TPU:4, one launch (start us, length us, event | category | flops | bytes accessed | tf_op | source)
XLA Modules:
  0.0 154.4 jit_solution(5176304205493552434)
XLA Ops:
  0.6 148.6 %panel_edit.1 = (f32[896,896]{1,0:T(8,128)}, f32[896,512]{1,0:T(8,128)}) custom-call(bf16[128,512]{1,0:T(8,128)(2,1)} %tok_ref.1, bf16[512,896]{1,0:T(8,128)(2,1)} %wg_ref.1, bf16[512,896]{1,0:T(8,128)(2,1)} %wu_ref.1, s32[1,8]{1,0:T(1,128)} %lengths_ref.1, s32[1,8]{1,0:T(1,128)} %raw_ref.1, f32[896]{0:T(1024)} %regular.1, bf16[128,512]{1,0:T(8,128)(2,1)} %res.1), custom_call_target="tpu_custom_call" | custom-call | tf_op jit(solution)/shard_map/panel_edit/pallas_call | solution.py:718
  149.2 0.0 copy-start
  149.2 3.9 %copy.11 = f32[896,896]{1,0:T(8,128)} copy(f32[896,896]{1,0:T(8,128)} %get-tuple-element.4) | data formatting | bytes 6422528
  153.1 0.0 copy-done
  153.1 1.2 copy.12
Async XLA Ops:
  149.2 3.9 %copy-start = (f32[896,512]{1,0:T(8,128)S(1)}, f32[896,512]{1,0:T(8,128)}, u32[]{:S(2)}) copy-start(f32[896,512]{1,0:T(8,128)} %get-tuple-element.5) | copy-start | bytes 5505028

commit v5 on v4

--- a/solution.py
+++ b/solution.py
@@ -140,7 +140,13 @@
         starts = starts + jnp.where(sub > j, jnp.broadcast_to(lengths[j:j + 1, :], (8, 128)), 0.0)
     wrapped = raw - lengths * jnp.floor((raw + 0.5) / lengths)
     spots[core, z] = starts + wrapped + ((z * 2 + core) * lanes).astype(f32)
-    pl.semaphore_wait(barrier, count)
+
+    @pl.when(holder)
+    def _():
+        for step in range(1, RING):
+            pl.semaphore_signal(barrier, inc=1, device_id=at_device(lax.rem(z + step, RING), core, 0, 0), device_id_type=MESH)
+
+    pl.semaphore_wait(barrier, count + jnp.where(origin, (RING - 1) * UNITS, 0))
 
     def spot_copy(dz):
         here = spots.at[core, z]
@@ -296,9 +302,9 @@
             packed(near_out.at[u, hop], g, v)
             near(u, hop).start()
 
-    def scatter(t):
-        return remote(kb.at[core * UNITS + t], k0.at[core * UNITS + t, rows_of(z)], ss.at[t], sr,
-                      at_device(z, core, 2 * core + t // COLS, lax.rem(t, COLS)))
+    def scatter(t, dz):
+        return remote(kb.at[core * UNITS + t], k0.at[core * UNITS + t, rows_of(z)], ss.at[t, dz], zr.at[dz],
+                      at_device(lax.rem(z + dz, RING), core, 2 * core + t // COLS, lax.rem(t, COLS)))
 
     def finish(u):
         g, v = own(u, z)
@@ -318,7 +324,12 @@
 
         @pl.when(jnp.logical_and(origin, jnp.logical_not(home)))
         def _():
-            scatter(t).start()
+            scatter(t, 0).start()
+
+        @pl.when(origin)
+        def _():
+            for dz in range(1, RING):
+                scatter(t, dz).start()
 
     def weights_here(j, _):
         rows = tile(j * 128, 128)
@@ -354,10 +365,6 @@
     n, tokens = k0.shape[1], 2 * UNITS * lanes
     half_rows = n // 2
 
-    def along(dz):
-        here = k0.at[core * UNITS + first, rows_of(z)]
-        return remote(here, here, zs.at[dz - 1], zr.at[dz - 1], at_device(lax.rem(z + dz, RING), core, row, col))
-
     def half_of(t, half):
         return k0.at[core * UNITS + t, pl.ds(half * half_rows, half_rows)]
 
@@ -396,16 +403,6 @@
 
     def here_block(t, half):
         remote(half_of(t, half), half_of(t, half), b1.at[0, 0], br.at[t, half], partner).wait_recv()
-
-    @pl.when(holder)
-    def _():
-        @pl.when(jnp.logical_not(jnp.logical_and(origin, core == 0)))
-        def _():
-            here = k0.at[core * UNITS + first, rows_of(z)]
-            remote(here, here, ss.at[0], sr, partner).wait_recv()
-
-        for dz in range(1, RING):
-            along(dz).start()
 
     for dz in range(1, RING):
         there = spots.at[core, lax.rem(z - dz + RING, RING)]
@@ -428,9 +425,16 @@
 
     @pl.when(holder)
     def _():
+        def piece_here(dz):
+            there = k0.at[core * UNITS + first, rows_of(lax.rem(z - dz + RING, RING))]
+            remote(there, there, zs.at[0], zr.at[dz], partner).wait_recv()
+
+        @pl.when(jnp.logical_not(jnp.logical_and(origin, core == 0)))
+        def _():
+            piece_here(0)
+
         for dz in range(1, RING):
-            there = k0.at[core * UNITS + first, rows_of(lax.rem(z - dz + RING, RING))]
-            remote(there, there, zs.at[dz - 1], zr.at[dz - 1], partner).wait_recv()
+            piece_here(dz)
         for step in (3, 1, 2):
             for half in range(2):
                 block_first(half, step).start()
@@ -649,9 +653,11 @@
             if t == 0:
                 @pl.when(core == 1)
                 def _():
-                    scatter(0).wait_send()
+                    scatter(0, 0).wait_send()
             else:
-                scatter(t).wait_send()
+                scatter(t, 0).wait_send()
+            for dz in range(1, RING):
+                scatter(t, dz).wait_send()
 
     for step in (1, 2, 3):
         token_first(step).wait_send()
@@ -666,8 +672,6 @@
 
     @pl.when(holder)
     def _():
-        for dz in range(1, RING):
-            along(dz).wait_send()
         for step in (1, 2, 3):
             for half in range(2):
                 block_first(half, step).wait_send()
@@ -748,7 +752,7 @@
             dma((3,)), dma((RING - 1,)), dma((RING - 1,)), dma, dma,
             dma((4,)), dma((2, 3)), dma((COLS, 3)), dma((UNITS, 2)), dma((tiles,)), dma((tiles,)),
             dma((UNITS, 4)), dma((UNITS, 4)), dma((UNITS, 3)), dma((UNITS, 3)),
-            dma, dma, dma((UNITS,)), dma, dma((RING - 1,)), dma((RING - 1,)),
+            dma, dma, dma((UNITS, RING)), dma, dma((RING - 1,)), dma((RING,)),
             dma((2, 3)), dma((2, 3)), dma((COLS, 3)), dma((UNITS, 2)),
             dma((2, 2)), dma((2, COLS)), dma((UNITS, 2, 2)), dma((UNITS,)), dma((UNITS,)),
             dma((RING - 1,)), dma((RING - 1,)), dma((RING - 1,)), dma((RING - 1,)), dma, dma,

time: 157 us -> 190 us (1.21)
  Pallas kernels: 149 us -> 181 us
    pallas_call x1, Pallas kernels: 149 us -> 181 us  [whole_call(): pl.pallas_call(whole_kernel, out_shape=[jax.ShapeDtypeStruct((n, n), f32)...]
where the time goes in v5:
time: 190 us; the launch traced here: 187 us
  Pallas kernels  181 us (95%)
  local copies, waits for them, and re-layouts  5.17 us (3%)
    pallas_call x1, Pallas kernels, whole_call(): pl.pallas_call(whole_kernel, out_shape=[jax.ShapeDtypeStruct((n, n), f32)...  181 us
    unnamed x4, local copies, waits for them, and re-layouts  5.17 us

profile of v5, /device:TPU:4, one launch (start us, length us, event | category | flops | bytes accessed | tf_op | source)
XLA Modules:
  0.0 186.6 jit_solution(7091584210183246960)
XLA Ops:
  0.6 180.8 %panel_edit.1 = (f32[896,896]{1,0:T(8,128)}, f32[896,512]{1,0:T(8,128)}) custom-call(bf16[128,512]{1,0:T(8,128)(2,1)} %tok_ref.1, bf16[512,896]{1,0:T(8,128)(2,1)} %wg_ref.1, bf16[512,896]{1,0:T(8,128)(2,1)} %wu_ref.1, s32[1,8]{1,0:T(1,128)} %lengths_ref.1, s32[1,8]{1,0:T(1,128)} %raw_ref.1, f32[896]{0:T(1024)} %regular.1, bf16[128,512]{1,0:T(8,128)(2,1)} %res.1), custom_call_target="tpu_custom_call" | custom-call | tf_op jit(solution)/shard_map/panel_edit/pallas_call | solution.py:722
  181.4 0.0 copy-start
  181.5 3.9 %copy.11 = f32[896,896]{1,0:T(8,128)} copy(f32[896,896]{1,0:T(8,128)} %get-tuple-element.4) | data formatting | bytes 6422528
  185.4 0.0 copy-done
  185.4 1.2 copy.12
Async XLA Ops:
  181.4 3.9 %copy-start = (f32[896,512]{1,0:T(8,128)S(1)}, f32[896,512]{1,0:T(8,128)}, u32[]{:S(2)}) copy-start(f32[896,512]{1,0:T(8,128)} %get-tuple-element.5) | copy-start | bytes 5505028
